TPU v7x, 32 devices: a whole 2x2x4 slice. The times are simulated.
32 devices in a mesh: section: 2 (over core), dp: 4 (over z), tensor: 4 (over y, x).
Axes of the slice: x: 2, y: 2, z: 4, core: 2. Of those that a mesh axis runs over, the one named last changes fastest.
Arguments:
- inputs: bfloat16 [4, 4, 1024, 640], P(None, 'dp', 'tensor'), may hold values from -6 to 6
- cotangent: bfloat16 [4, 4, 1024, 640], P(None, 'dp', 'tensor'), may hold values from -6 to 6
- pre_attn_gain: bfloat16 [2, 640], P('section', 'dp'), may hold values from 0.25 to 1.75
- post_attn_gain: bfloat16 [2, 640], P('section', 'dp'), may hold values from 0.25 to 1.75
- pre_ffn_gain: bfloat16 [2, 640], P('section', 'dp'), may hold values from 0.25 to 1.75
- post_ffn_gain: bfloat16 [2, 640], P('section', 'dp'), may hold values from 0.25 to 1.75
- query_gain: bfloat16 [2, 256], P('section', 'dp'), may hold values from 0.25 to 1.75
- key_gain: bfloat16 [2, 256], P('section', 'dp'), may hold values from 0.25 to 1.75
- query_weight: bfloat16 [2, 640, 1024], P('section', 'dp', 'tensor'), may hold values from -0.25 to 0.25
- key_weight: bfloat16 [2, 640, 256], P('section', 'dp'), may hold values from -0.25 to 0.25
- value_weight: bfloat16 [2, 640, 256], P('section', 'dp'), may hold values from -0.25 to 0.25
- out_weight: bfloat16 [2, 1024, 640], P('section', 'tensor', 'dp'), may hold values from -0.1875 to 0.1875
- gate_weight: bfloat16 [2, 640, 2048], P('section', 'dp', 'tensor'), may hold values from -0.25 to 0.25
- up_weight: bfloat16 [2, 640, 2048], P('section', 'dp', 'tensor'), may hold values from -0.25 to 0.25
- down_weight: bfloat16 [2, 2048, 640], P('section', 'tensor', 'dp'), may hold values from -0.125 to 0.125
Outputs:
- layer_outputs: bfloat16 [2, 4, 4, 1024, 640], P('section', None, 'dp', 'tensor')
- input_grads: float32 [2, 4, 4, 1024, 640], P('section', None, 'dp', 'tensor')
- grad_pre_attn_gain: float32 [2, 640], P('section', 'dp')
- grad_post_attn_gain: float32 [2, 640], P('section', 'dp')
- grad_pre_ffn_gain: float32 [2, 640], P('section', 'dp')
- grad_post_ffn_gain: float32 [2, 640], P('section', 'dp')
- grad_query_gain: float32 [2, 256], P('section', 'dp')
- grad_key_gain: float32 [2, 256], P('section', 'dp')
- grad_query_weight: float32 [2, 640, 1024], P('section', 'dp', 'tensor')
- grad_key_weight: float32 [2, 640, 256], P('section', 'dp')
- grad_value_weight: float32 [2, 640, 256], P('section', 'dp')
- grad_out_weight: float32 [2, 1024, 640], P('section', 'tensor', 'dp')
- grad_gate_weight: float32 [2, 640, 2048], P('section', 'dp', 'tensor')
- grad_up_weight: float32 [2, 640, 2048], P('section', 'dp', 'tensor')
- grad_down_weight: float32 [2, 2048, 640], P('section', 'tensor', 'dp')
All inputs are finite; a program needn't handle non-finite values.
Results may differ from a plain program's by a relative error of at most 0.038.
Values may be sent and summed in bfloat16 or wider, within the bound.
A program may use at most 256 MiB of HBM per device.

v0:
```python
from functools import partial
import math

import jax
import jax.numpy as jnp
from jax import lax
from jax.sharding import PartitionSpec as P

WIN = 512


EPSILON = 1e-06
NEGATIVE = -1e30


def from_behind(block, axis, distance):
    devices = range(lax.axis_size(axis))
    route = [(i - distance, i) for i in devices if i - distance in devices]
    return lax.ppermute(block, axis, route)


def norm_gain(values, scales):
    return values * lax.rsqrt(jnp.mean(values * values, axis=-1, keepdims=True) + EPSILON) * scales


def rotary_tables(length, dimension):
    halved = dimension // 2
    positions = jnp.arange(length, dtype=jnp.int32).astype(jnp.float32)
    indices = jnp.arange(halved, dtype=jnp.int32).astype(jnp.float32)
    inverse = jnp.exp(indices * (-2.0 * math.log(10000.0) / dimension))
    angles = positions[:, None] * inverse[None, :]
    return (jnp.cos(angles), jnp.sin(angles))


def rotate(values, cosine_table, sine_table):
    halved = values.shape[-1] // 2
    former = values[..., :halved]
    latter = values[..., halved:]
    return jnp.concatenate(
        [former * cosine_table - latter * sine_table, latter * cosine_table + former * sine_table],
        axis=-1,
    )


def query_path(raw_values, scales, cosine_table, sine_table):
    return rotate(norm_gain(raw_values, scales), cosine_table, sine_table) * raw_values.shape[
        -1
    ] ** (-0.5)


def key_path(raw_values, scales, cosine_table, sine_table):
    return rotate(norm_gain(raw_values, scales), cosine_table, sine_table)


def gated_unit(gate_proj, projected_up):
    return jax.nn.gelu(gate_proj, approximate=True) * projected_up


def spread_rows(local_rows):
    return lax.all_gather(local_rows, "tensor", axis=1, tiled=True)


def fold_rows(partial_rows):
    return lax.psum_scatter(
        partial_rows.astype(jnp.bfloat16), "tensor", scatter_dimension=1, tiled=True
    ).astype(jnp.float32)


def spread_grads(local_rows):
    return lax.all_gather(local_rows, "tensor", axis=1, tiled=True)


def fold_grads(partial_rows):
    return lax.psum_scatter(
        partial_rows.astype(jnp.bfloat16), "tensor", scatter_dimension=1, tiled=True
    ).astype(jnp.float32)


def fetch_weights(shards):
    return (
        lax.all_gather(shards[0], "dp", axis=0, tiled=True),
        lax.all_gather(shards[1], "dp", axis=0, tiled=True),
        lax.all_gather(shards[2], "dp", axis=0, tiled=True),
        lax.all_gather(shards[3], "dp", axis=0, tiled=True),
        lax.all_gather(shards[4], "dp", axis=0, tiled=True),
        lax.all_gather(shards[5], "dp", axis=0, tiled=True),
        lax.all_gather(shards[6], "dp", axis=0, tiled=True),
        lax.all_gather(shards[7], "dp", axis=0, tiled=True),
        lax.all_gather(shards[8], "dp", axis=0, tiled=True),
        lax.all_gather(shards[9], "dp", axis=1, tiled=True),
        lax.all_gather(shards[10], "dp", axis=0, tiled=True),
        lax.all_gather(shards[11], "dp", axis=0, tiled=True),
        lax.all_gather(shards[12], "dp", axis=1, tiled=True),
    )


def reduce_weights(grads_full):
    return (
        lax.psum_scatter(
            grads_full[0].astype(jnp.bfloat16), "dp", scatter_dimension=0, tiled=True
        ).astype(jnp.float32),
        lax.psum_scatter(
            grads_full[1].astype(jnp.bfloat16), "dp", scatter_dimension=0, tiled=True
        ).astype(jnp.float32),
        lax.psum_scatter(
            grads_full[2].astype(jnp.bfloat16), "dp", scatter_dimension=0, tiled=True
        ).astype(jnp.float32),
        lax.psum_scatter(
            grads_full[3].astype(jnp.bfloat16), "dp", scatter_dimension=0, tiled=True
        ).astype(jnp.float32),
        lax.psum_scatter(
            grads_full[4].astype(jnp.bfloat16), "dp", scatter_dimension=0, tiled=True
        ).astype(jnp.float32),
        lax.psum_scatter(
            grads_full[5].astype(jnp.bfloat16), "dp", scatter_dimension=0, tiled=True
        ).astype(jnp.float32),
        lax.psum_scatter(
            grads_full[6].astype(jnp.bfloat16), "dp", scatter_dimension=0, tiled=True
        ).astype(jnp.float32),
        lax.psum_scatter(
            grads_full[7].astype(jnp.bfloat16), "dp", scatter_dimension=0, tiled=True
        ).astype(jnp.float32),
        lax.psum_scatter(
            grads_full[8].astype(jnp.bfloat16), "dp", scatter_dimension=0, tiled=True
        ).astype(jnp.float32),
        lax.psum_scatter(
            grads_full[9].astype(jnp.bfloat16), "dp", scatter_dimension=1, tiled=True
        ).astype(jnp.float32),
        lax.psum_scatter(
            grads_full[10].astype(jnp.bfloat16), "dp", scatter_dimension=0, tiled=True
        ).astype(jnp.float32),
        lax.psum_scatter(
            grads_full[11].astype(jnp.bfloat16), "dp", scatter_dimension=0, tiled=True
        ).astype(jnp.float32),
        lax.psum_scatter(
            grads_full[12].astype(jnp.bfloat16), "dp", scatter_dimension=1, tiled=True
        ).astype(jnp.float32),
    )


def score_block(queries, keys_padded, offset, block_rows):
    query_block = lax.slice_in_dim(queries, offset, offset + block_rows, axis=1)
    key_block = lax.slice_in_dim(keys_padded, offset, offset + block_rows + WIN, axis=1)
    scores = jnp.einsum(
        "sqhd,skd->shqk", query_block, key_block, preferred_element_type=jnp.float32
    )
    query_pos = offset + jnp.arange(block_rows, dtype=jnp.int32)
    key_pos = offset - WIN + jnp.arange(block_rows + WIN, dtype=jnp.int32)
    allowed = (
        (key_pos[None, :] >= 0)
        & (key_pos[None, :] <= query_pos[:, None])
        & (query_pos[:, None] - key_pos[None, :] < WIN)
    )
    return (jnp.where(allowed, scores, NEGATIVE), query_block, key_block)


def attend_forward(queries, keys_all, values_all):
    length = queries.shape[1]
    block_rows = min(512, length)
    padding = ((0, 0), (WIN, 0), (0, 0))
    keys_padded = jnp.pad(keys_all, padding)
    values_padded = jnp.pad(values_all, padding)
    outputs = []
    log_totals = []
    for offset in range(0, length, block_rows):
        scores, query_block, key_block = score_block(queries, keys_padded, offset, block_rows)
        highest = jnp.max(scores, axis=-1, keepdims=True)
        log_total = highest + jnp.log(jnp.sum(jnp.exp(scores - highest), axis=-1, keepdims=True))
        weights = jnp.exp(scores - log_total).astype(jnp.bfloat16)
        value_block = lax.slice_in_dim(values_padded, offset, offset + block_rows + WIN, axis=1)
        outputs.append(
            jnp.einsum("shqk,skd->sqhd", weights, value_block, preferred_element_type=jnp.float32)
        )
        log_totals.append(log_total)
    return (jnp.concatenate(outputs, axis=1), log_totals)


def attend_backward(queries, keys_all, values_all, log_totals, attended_grad):
    length = queries.shape[1]
    block_rows = min(512, length)
    padding = ((0, 0), (WIN, 0), (0, 0))
    keys_padded = jnp.pad(keys_all, padding)
    values_padded = jnp.pad(values_all, padding)
    query_grads = []
    key_grad = jnp.zeros(keys_padded.shape, jnp.float32)
    value_sum = jnp.zeros(values_padded.shape, jnp.float32)
    for number, offset in enumerate(range(0, length, block_rows)):
        scores, query_block, key_block = score_block(queries, keys_padded, offset, block_rows)
        weights = jnp.exp(scores - log_totals[number])
        value_block = lax.slice_in_dim(values_padded, offset, offset + block_rows + WIN, axis=1)
        grad_block = lax.slice_in_dim(attended_grad, offset, offset + block_rows, axis=1)
        probs_grad = jnp.einsum(
            "sqhd,skd->shqk", grad_block, value_block, preferred_element_type=jnp.float32
        )
        row_inner = jnp.sum(weights * probs_grad, axis=-1, keepdims=True)
        score_grad = (weights * (probs_grad - row_inner)).astype(jnp.bfloat16)
        query_grads.append(
            jnp.einsum("shqk,skd->sqhd", score_grad, key_block, preferred_element_type=jnp.float32)
        )
        placing = ((0, 0), (offset, length - offset - block_rows), (0, 0))
        key_grad = key_grad + jnp.pad(
            jnp.einsum(
                "shqk,sqhd->skd", score_grad, query_block, preferred_element_type=jnp.float32
            ),
            placing,
        )
        value_sum = value_sum + jnp.pad(
            jnp.einsum(
                "shqk,sqhd->skd",
                weights.astype(jnp.bfloat16),
                grad_block,
                preferred_element_type=jnp.float32,
            ),
            placing,
        )
    return (jnp.concatenate(query_grads, axis=1), key_grad[:, WIN:], value_sum[:, WIN:])


def forward(inputs, layer_weights):
    (
        pre_attn,
        post_attn,
        pre_ffn,
        post_ffn,
        query_scale,
        key_scale,
        projected_queries,
        projected_keys,
        projected_values,
        output_projected,
        gate_weight_matrix,
        up_weight_matrix,
        down_weight_matrix,
    ) = layer_weights
    normalized_rows = spread_rows(
        norm_gain(inputs, pre_attn.astype(jnp.float32)).astype(jnp.bfloat16)
    )
    seq_count = normalized_rows.shape[0]
    length = normalized_rows.shape[1]
    head_size = projected_keys.shape[1]
    head_count = projected_queries.shape[1] // head_size
    cosine_table, sine_table = rotary_tables(length, head_size)
    query_raw = jnp.einsum(
        "xmv,vn->xmn", normalized_rows, projected_queries, preferred_element_type=jnp.float32
    ).reshape(seq_count, length, head_count, head_size)
    unrotated_keys = jnp.einsum(
        "xmv,vn->xmn", normalized_rows, projected_keys, preferred_element_type=jnp.float32
    )
    values_all = jnp.einsum(
        "xmv,vn->xmn", normalized_rows, projected_values, preferred_element_type=jnp.float32
    ).astype(jnp.bfloat16)
    queries = query_path(
        query_raw, query_scale.astype(jnp.float32), cosine_table[:, None, :], sine_table[:, None, :]
    ).astype(jnp.bfloat16)
    keys_all = key_path(
        unrotated_keys, key_scale.astype(jnp.float32), cosine_table, sine_table
    ).astype(jnp.bfloat16)
    attention_out, log_totals = attend_forward(queries, keys_all, values_all)
    attended_rows = attention_out.reshape(seq_count, length, head_count * head_size).astype(
        jnp.bfloat16
    )
    branch = fold_rows(
        jnp.einsum(
            "ovi,iw->ovw", attended_rows, output_projected, preferred_element_type=jnp.float32
        )
    )
    hidden = inputs + norm_gain(branch, post_attn.astype(jnp.float32))
    feedforward_input = spread_rows(
        norm_gain(hidden, pre_ffn.astype(jnp.float32)).astype(jnp.bfloat16)
    )
    gate_proj = jnp.einsum(
        "hra,ay->hry", feedforward_input, gate_weight_matrix, preferred_element_type=jnp.float32
    )
    projected_up = jnp.einsum(
        "hra,ay->hry", feedforward_input, up_weight_matrix, preferred_element_type=jnp.float32
    )
    gated_product = gated_unit(gate_proj, projected_up).astype(jnp.bfloat16)
    ffn_output = fold_rows(
        jnp.einsum(
            "cep,pz->cez", gated_product, down_weight_matrix, preferred_element_type=jnp.float32
        )
    )
    result = hidden + norm_gain(ffn_output, post_ffn.astype(jnp.float32))
    kept_values = (
        inputs,
        normalized_rows,
        query_raw,
        unrotated_keys,
        queries,
        keys_all,
        values_all,
        log_totals,
        attended_rows,
        branch,
        hidden,
        feedforward_input,
        gate_proj,
        projected_up,
        gated_product,
        ffn_output,
    )
    return (result, kept_values)


def backward(grad_output, kept_values, layer_weights):
    (
        pre_attn,
        post_attn,
        pre_ffn,
        post_ffn,
        query_scale,
        key_scale,
        projected_queries,
        projected_keys,
        projected_values,
        output_projected,
        gate_weight_matrix,
        up_weight_matrix,
        down_weight_matrix,
    ) = layer_weights
    (
        inputs,
        normalized_rows,
        query_raw,
        unrotated_keys,
        queries,
        keys_all,
        values_all,
        log_totals,
        attended_rows,
        branch,
        hidden,
        feedforward_input,
        gate_proj,
        projected_up,
        gated_product,
        ffn_output,
    ) = kept_values
    seq_count, length, head_count, head_size = queries.shape
    pull_post = jax.vjp(norm_gain, ffn_output, post_ffn.astype(jnp.float32))[1]
    output_grad, post_ffn_grad = pull_post(grad_output)
    down_side_input = spread_grads(output_grad.astype(jnp.bfloat16))
    product_grad = jnp.einsum(
        "ckg,vg->ckv", down_side_input, down_weight_matrix, preferred_element_type=jnp.float32
    )
    down_output_grad = jnp.einsum(
        "pnk,png->kg", gated_product, down_side_input, preferred_element_type=jnp.float32
    )
    pull_gated = jax.vjp(gated_unit, gate_proj, projected_up)[1]
    gate_output_grad, up_output_grad = pull_gated(product_grad)
    gate_output_grad = gate_output_grad.astype(jnp.bfloat16)
    up_output_grad = up_output_grad.astype(jnp.bfloat16)
    gate_matrix_grad = jnp.einsum(
        "xkc,xki->ci", feedforward_input, gate_output_grad, preferred_element_type=jnp.float32
    )
    up_matrix_grad = jnp.einsum(
        "xkc,xki->ci", feedforward_input, up_output_grad, preferred_element_type=jnp.float32
    )
    ffn_input_grad = fold_grads(
        jnp.einsum(
            "kqt,mt->kqm", gate_output_grad, gate_weight_matrix, preferred_element_type=jnp.float32
        )
        + jnp.einsum(
            "kqt,mt->kqm", up_output_grad, up_weight_matrix, preferred_element_type=jnp.float32
        )
    )
    pull_pre = jax.vjp(norm_gain, hidden, pre_ffn.astype(jnp.float32))[1]
    hidden_part, pre_ffn_grad = pull_pre(ffn_input_grad)
    hidden_grad = grad_output + hidden_part
    pull_branch = jax.vjp(norm_gain, branch, post_attn.astype(jnp.float32))[1]
    branch_grad, post_attn_grad = pull_branch(hidden_grad)
    output_side_input = spread_grads(branch_grad.astype(jnp.bfloat16))
    attended_grad = jnp.einsum(
        "iyx,zx->iyz", output_side_input, output_projected, preferred_element_type=jnp.float32
    ).astype(jnp.bfloat16)
    out_proj_grad = jnp.einsum(
        "xkj,xkw->jw", attended_rows, output_side_input, preferred_element_type=jnp.float32
    )
    query_grad, key_grad, value_sum = attend_backward(
        queries,
        keys_all,
        values_all,
        log_totals,
        attended_grad.reshape(seq_count, length, head_count, head_size),
    )
    value_rows_grad = value_sum.astype(jnp.bfloat16)
    cosine_table, sine_table = rotary_tables(length, head_size)
    pull_query = jax.vjp(
        partial(
            query_path, cosine_table=cosine_table[:, None, :], sine_table=sine_table[:, None, :]
        ),
        query_raw,
        query_scale.astype(jnp.float32),
    )[1]
    unrotated_query_grad, query_scale_grad = pull_query(query_grad)
    unrotated_query_grad = unrotated_query_grad.reshape(
        seq_count, length, head_count * head_size
    ).astype(jnp.bfloat16)
    pull_key = jax.vjp(
        partial(key_path, cosine_table=cosine_table, sine_table=sine_table),
        unrotated_keys,
        key_scale.astype(jnp.float32),
    )[1]
    unrotated_key_grad, key_scale_grad = pull_key(key_grad)
    unrotated_key_grad = unrotated_key_grad.astype(jnp.bfloat16)
    query_proj_grad = jnp.einsum(
        "mfo,mfb->ob", normalized_rows, unrotated_query_grad, preferred_element_type=jnp.float32
    )
    key_proj_grad = jnp.einsum(
        "mfo,mfb->ob", normalized_rows, unrotated_key_grad, preferred_element_type=jnp.float32
    )
    value_proj_grad = jnp.einsum(
        "mfo,mfb->ob", normalized_rows, value_rows_grad, preferred_element_type=jnp.float32
    )
    normed_terms = jnp.einsum(
        "ptc,jc->ptj", unrotated_query_grad, projected_queries, preferred_element_type=jnp.float32
    )
    normed_terms = normed_terms + jnp.einsum(
        "ptc,jc->ptj", unrotated_key_grad, projected_keys, preferred_element_type=jnp.float32
    )
    normed_terms = normed_terms + jnp.einsum(
        "ptc,jc->ptj", value_rows_grad, projected_values, preferred_element_type=jnp.float32
    )
    normed_grad = fold_grads(normed_terms)
    pull_input = jax.vjp(norm_gain, inputs, pre_attn.astype(jnp.float32))[1]
    input_part, pre_attn_grad = pull_input(normed_grad)
    input_grad = hidden_grad + input_part
    return (
        input_grad,
        (
            pre_attn_grad,
            post_attn_grad,
            pre_ffn_grad,
            post_ffn_grad,
            query_scale_grad,
            key_scale_grad,
            query_proj_grad,
            key_proj_grad,
            value_proj_grad,
            out_proj_grad,
            gate_matrix_grad,
            up_matrix_grad,
            down_output_grad,
        ),
    )


def local(
    inputs,
    cotangent,
    pre_attn_gain,
    post_attn_gain,
    pre_ffn_gain,
    post_ffn_gain,
    query_gain,
    key_gain,
    query_weight,
    key_weight,
    value_weight,
    out_weight,
    gate_weight,
    up_weight,
    down_weight,
):
    section_index = lax.axis_index("section")
    first_section = section_index == 0
    shards = (
        pre_attn_gain[0],
        post_attn_gain[0],
        pre_ffn_gain[0],
        post_ffn_gain[0],
        query_gain[0],
        key_gain[0],
        query_weight[0],
        key_weight[0],
        value_weight[0],
        out_weight[0],
        gate_weight[0],
        up_weight[0],
        down_weight[0],
    )
    micro_count = inputs.shape[0]
    results = []
    saved_ticks = []
    arrived = jnp.zeros(inputs.shape[1:], jnp.bfloat16)
    for tick_index in range(micro_count + 1):
        layer_weights = fetch_weights(shards)
        own_input = inputs[min(tick_index, micro_count - 1)]
        current = jnp.where(first_section, own_input, arrived).astype(jnp.float32)
        result, kept_values = forward(current, layer_weights)
        rounded = result.astype(jnp.bfloat16)
        results.append(rounded)
        saved_ticks.append(kept_values)
        if tick_index < micro_count:
            arrived = from_behind(rounded, "section", 1)
    returned = jnp.zeros(inputs.shape[1:], jnp.bfloat16)
    grad_pairs = []
    summed = None
    for turn_index in range(micro_count + 1):
        layer_weights = fetch_weights(shards)
        if turn_index < micro_count:
            supplied = cotangent[micro_count - 1 - turn_index].astype(jnp.float32)
        else:
            supplied = jnp.zeros(inputs.shape[1:], jnp.float32)
        grad_output = jnp.where(first_section, returned.astype(jnp.float32), supplied)
        input_grad, tick_grads = backward(
            grad_output, saved_ticks[micro_count - turn_index], layer_weights
        )
        rounded_grad = input_grad.astype(jnp.bfloat16)
        grad_pairs.append((input_grad, rounded_grad))
        if turn_index < micro_count:
            returned = from_behind(rounded_grad, "section", -1)
        contribution = reduce_weights(tick_grads)
        summed = (
            contribution
            if summed is None
            else tuple((earlier + later for earlier, later in zip(summed, contribution)))
        )
    shared = (
        lax.psum(summed[0].astype(jnp.bfloat16), "tensor").astype(jnp.float32),
        lax.psum(summed[1].astype(jnp.bfloat16), "tensor").astype(jnp.float32),
        lax.psum(summed[2].astype(jnp.bfloat16), "tensor").astype(jnp.float32),
        lax.psum(summed[3].astype(jnp.bfloat16), "tensor").astype(jnp.float32),
        lax.psum(summed[4].astype(jnp.bfloat16), "tensor").astype(jnp.float32),
        lax.psum(summed[5].astype(jnp.bfloat16), "tensor").astype(jnp.float32),
        lax.psum(summed[7].astype(jnp.bfloat16), "tensor").astype(jnp.float32),
        lax.psum(summed[8].astype(jnp.bfloat16), "tensor").astype(jnp.float32),
    )
    finished = (
        shared[0],
        shared[1],
        shared[2],
        shared[3],
        shared[4],
        shared[5],
        summed[6],
        shared[6],
        shared[7],
        summed[9],
        summed[10],
        summed[11],
        summed[12],
    )
    layer_outputs = jnp.stack(
        [
            jnp.where(first_section, results[batch_index], results[batch_index + 1])
            for batch_index in range(micro_count)
        ]
    )[None]
    input_grads = jnp.stack(
        [
            jnp.where(
                first_section,
                grad_pairs[micro_count - batch_index][0],
                grad_pairs[micro_count - 1 - batch_index][1].astype(jnp.float32),
            )
            for batch_index in range(micro_count)
        ]
    )[None]
    return (layer_outputs, input_grads) + tuple((gradient[None] for gradient in finished))


def solution(mesh):
    return jax.shard_map(
        local,
        mesh=mesh,
        in_specs=(
            P(None, "dp", "tensor", None),
            P(None, "dp", "tensor", None),
            P("section", "dp"),
            P("section", "dp"),
            P("section", "dp"),
            P("section", "dp"),
            P("section", "dp"),
            P("section", "dp"),
            P("section", "dp", "tensor"),
            P("section", "dp", None),
            P("section", "dp", None),
            P("section", "tensor", "dp"),
            P("section", "dp", "tensor"),
            P("section", "dp", "tensor"),
            P("section", "tensor", "dp"),
        ),
        out_specs=(
            P("section", None, "dp", "tensor", None),
            P("section", None, "dp", "tensor", None),
            P("section", "dp"),
            P("section", "dp"),
            P("section", "dp"),
            P("section", "dp"),
            P("section", "dp"),
            P("section", "dp"),
            P("section", "dp", "tensor"),
            P("section", "dp", None),
            P("section", "dp", None),
            P("section", "tensor", "dp"),
            P("section", "dp", "tensor"),
            P("section", "dp", "tensor"),
            P("section", "tensor", "dp"),
        ),
        check_vma=False,
    )
```

profile of v0, /device:TPU:0, one launch (start us, length us, event | category | flops | bytes accessed | tf_op | source)
XLA Modules:
  0.0 2479.1 jit_solution(9919820242527013391)
XLA Ops:
  104.8 28.2 %reduce-scatter.56.cloned.1.call-done = bf16[1,256,640]{2,1,0:T(8,128)(2,1)} async-done(((bf16[1,1024,640]{2,1,0:T(8,128)(2,1)}), bf16[1,256,640]{2,1,0:T(8,128)(2,1)}) %reduce-scatter.56.cloned.1.call-update) | async-done | bytes 327696 | tf_op jit(solution)/shard_map/reduce_scatter | solution.py:64
  199.0 28.8 %reduce-scatter.58.cloned.1.call-done = bf16[1,256,640]{2,1,0:T(8,128)(2,1)} async-done(((bf16[1,1024,640]{2,1,0:T(8,128)(2,1)}), bf16[1,256,640]{2,1,0:T(8,128)(2,1)}) %reduce-scatter.58.cloned.1.call-update) | async-done | bytes 327696 | tf_op jit(solution)/shard_map/reduce_scatter | solution.py:64
  235.4 28.9 %all-gather.38.cloned.1.call-done = bf16[1,1024,640]{2,1,0:T(8,128)(2,1)} async-done(((bf16[1,256,640]{2,1,0:T(8,128)(2,1)}), bf16[1,1024,640]{2,1,0:T(8,128)(2,1)}) %all-gather.38.cloned.1.call-update) | async-done | bytes 1310736 | tf_op jit(solution)/shard_map/all_gather | solution.py:60
  278.7 29.4 %reduce-scatter.60.cloned.1.call-done = bf16[1,256,640]{2,1,0:T(8,128)(2,1)} async-done(((bf16[1,1024,640]{2,1,0:T(8,128)(2,1)}), bf16[1,256,640]{2,1,0:T(8,128)(2,1)}) %reduce-scatter.60.cloned.1.call-update) | async-done | bytes 327696 | tf_op jit(solution)/shard_map/reduce_scatter | solution.py:64
  313.6 28.5 %all-gather.40.cloned.1.call-done = bf16[1,1024,640]{2,1,0:T(8,128)(2,1)} async-done(((bf16[1,256,640]{2,1,0:T(8,128)(2,1)}), bf16[1,1024,640]{2,1,0:T(8,128)(2,1)}) %all-gather.40.cloned.1.call-update) | async-done | bytes 1310736 | tf_op jit(solution)/shard_map/all_gather | solution.py:60
  350.3 29.4 %reduce-scatter.62.cloned.1.call-done = bf16[1,256,640]{2,1,0:T(8,128)(2,1)} async-done(((bf16[1,1024,640]{2,1,0:T(8,128)(2,1)}), bf16[1,256,640]{2,1,0:T(8,128)(2,1)}) %reduce-scatter.62.cloned.1.call-update) | async-done | bytes 327696 | tf_op jit(solution)/shard_map/reduce_scatter | solution.py:64
  388.1 29.0 %all-gather.42.cloned.1.call-done = bf16[1,1024,640]{2,1,0:T(8,128)(2,1)} async-done(((bf16[1,256,640]{2,1,0:T(8,128)(2,1)}), bf16[1,1024,640]{2,1,0:T(8,128)(2,1)}) %all-gather.42.cloned.1.call-update) | async-done | bytes 1310736 | tf_op jit(solution)/shard_map/all_gather | solution.py:60
  432.4 29.4 %reduce-scatter.64.cloned.1.call-done = bf16[1,256,640]{2,1,0:T(8,128)(2,1)} async-done(((bf16[1,1024,640]{2,1,0:T(8,128)(2,1)}), bf16[1,256,640]{2,1,0:T(8,128)(2,1)}) %reduce-scatter.64.cloned.1.call-update) | async-done | bytes 327696 | tf_op jit(solution)/shard_map/reduce_scatter | solution.py:64
  466.4 28.7 %all-gather.44.cloned.1.call-done = bf16[1,1024,640]{2,1,0:T(8,128)(2,1)} async-done(((bf16[1,256,640]{2,1,0:T(8,128)(2,1)}), bf16[1,1024,640]{2,1,0:T(8,128)(2,1)}) %all-gather.44.cloned.1.call-update) | async-done | bytes 1310736 | tf_op jit(solution)/shard_map/all_gather | solution.py:60
  503.6 29.5 %reduce-scatter.66.cloned.1.call-done = bf16[1,256,640]{2,1,0:T(8,128)(2,1)} async-done(((bf16[1,1024,640]{2,1,0:T(8,128)(2,1)}), bf16[1,256,640]{2,1,0:T(8,128)(2,1)}) %reduce-scatter.66.cloned.1.call-update) | async-done | bytes 327696 | tf_op jit(solution)/shard_map/reduce_scatter | solution.py:64
  541.4 28.9 %all-gather.46.cloned.1.call-done = bf16[1,1024,640]{2,1,0:T(8,128)(2,1)} async-done(((bf16[1,256,640]{2,1,0:T(8,128)(2,1)}), bf16[1,1024,640]{2,1,0:T(8,128)(2,1)}) %all-gather.46.cloned.1.call-update) | async-done | bytes 1310736 | tf_op jit(solution)/shard_map/all_gather | solution.py:60
  585.7 29.4 %reduce-scatter.68.cloned.1.call-done = bf16[1,256,640]{2,1,0:T(8,128)(2,1)} async-done(((bf16[1,1024,640]{2,1,0:T(8,128)(2,1)}), bf16[1,256,640]{2,1,0:T(8,128)(2,1)}) %reduce-scatter.68.cloned.1.call-update) | async-done | bytes 327696 | tf_op jit(solution)/shard_map/reduce_scatter | solution.py:64
  619.8 28.7 %all-gather.48.cloned.1.call-done = bf16[1,1024,640]{2,1,0:T(8,128)(2,1)} async-done(((bf16[1,256,640]{2,1,0:T(8,128)(2,1)}), bf16[1,1024,640]{2,1,0:T(8,128)(2,1)}) %all-gather.48.cloned.1.call-update) | async-done | bytes 1310736 | tf_op jit(solution)/shard_map/all_gather | solution.py:60
  656.9 29.5 %reduce-scatter.70.cloned.1.call-done = bf16[1,256,640]{2,1,0:T(8,128)(2,1)} async-done(((bf16[1,1024,640]{2,1,0:T(8,128)(2,1)}), bf16[1,256,640]{2,1,0:T(8,128)(2,1)}) %reduce-scatter.70.cloned.1.call-update) | async-done | bytes 327696 | tf_op jit(solution)/shard_map/reduce_scatter | solution.py:64
  694.7 28.9 %all-gather.50.cloned.1.call-done = bf16[1,1024,640]{2,1,0:T(8,128)(2,1)} async-done(((bf16[1,256,640]{2,1,0:T(8,128)(2,1)}), bf16[1,1024,640]{2,1,0:T(8,128)(2,1)}) %all-gather.50.cloned.1.call-update) | async-done | bytes 1310736 | tf_op jit(solution)/shard_map/all_gather | solution.py:60
  739.3 29.4 %reduce-scatter.72.cloned.1.call-done = bf16[1,256,640]{2,1,0:T(8,128)(2,1)} async-done(((bf16[1,1024,640]{2,1,0:T(8,128)(2,1)}), bf16[1,256,640]{2,1,0:T(8,128)(2,1)}) %reduce-scatter.72.cloned.1.call-update) | async-done | bytes 327696 | tf_op jit(solution)/shard_map/reduce_scatter | solution.py:64
  774.8 28.5 %all-gather.52.cloned.1.call-done = bf16[1,1024,640]{2,1,0:T(8,128)(2,1)} async-done(((bf16[1,256,640]{2,1,0:T(8,128)(2,1)}), bf16[1,1024,640]{2,1,0:T(8,128)(2,1)}) %all-gather.52.cloned.1.call-update) | async-done | bytes 1310736 | tf_op jit(solution)/shard_map/all_gather | solution.py:60
  811.7 29.4 %reduce-scatter.74.cloned.1.call-done = bf16[1,256,640]{2,1,0:T(8,128)(2,1)} async-done(((bf16[1,1024,640]{2,1,0:T(8,128)(2,1)}), bf16[1,256,640]{2,1,0:T(8,128)(2,1)}) %reduce-scatter.74.cloned.1.call-update) | async-done | bytes 327696 | tf_op jit(solution)/shard_map/reduce_scatter | solution.py:64
  846.3 28.9 %all-gather.54.cloned.1.call-done = bf16[1,1024,640]{2,1,0:T(8,128)(2,1)} async-done(((bf16[1,256,640]{2,1,0:T(8,128)(2,1)}), bf16[1,1024,640]{2,1,0:T(8,128)(2,1)}) %all-gather.54.cloned.1.call-update) | async-done | bytes 1310736 | tf_op jit(solution)/shard_map/all_gather | solution.py:70
  884.2 29.5 %reduce-scatter.76.cloned.1.call-done = bf16[1,256,640]{2,1,0:T(8,128)(2,1)} async-done(((bf16[1,1024,640]{2,1,0:T(8,128)(2,1)}), bf16[1,256,640]{2,1,0:T(8,128)(2,1)}) %reduce-scatter.76.cloned.1.call-update) | async-done | bytes 327696 | tf_op jit(solution)/shard_map/reduce_scatter | solution.py:74
  920.9 28.7 %all-gather.56.cloned.1.call-done = bf16[1,1024,640]{2,1,0:T(8,128)(2,1)} async-done(((bf16[1,256,640]{2,1,0:T(8,128)(2,1)}), bf16[1,1024,640]{2,1,0:T(8,128)(2,1)}) %all-gather.56.cloned.1.call-update) | async-done | bytes 1310736 | tf_op jit(solution)/shard_map/all_gather | solution.py:70
  972.0 29.4 %reduce-scatter.78.cloned.1.call-done = bf16[1,256,640]{2,1,0:T(8,128)(2,1)} async-done(((bf16[1,1024,640]{2,1,0:T(8,128)(2,1)}), bf16[1,256,640]{2,1,0:T(8,128)(2,1)}) %reduce-scatter.78.cloned.1.call-update) | async-done | bytes 327696 | tf_op jit(solution)/shard_map/reduce_scatter | solution.py:74
  1010.2 28.9 %all-gather.58.cloned.1.call-done = bf16[1,1024,640]{2,1,0:T(8,128)(2,1)} async-done(((bf16[1,256,640]{2,1,0:T(8,128)(2,1)}), bf16[1,1024,640]{2,1,0:T(8,128)(2,1)}) %all-gather.58.cloned.1.call-update) | async-done | bytes 1310736 | tf_op jit(solution)/shard_map/all_gather | solution.py:70
  1048.1 29.5 %reduce-scatter.80.cloned.1.call-done = bf16[1,256,640]{2,1,0:T(8,128)(2,1)} async-done(((bf16[1,1024,640]{2,1,0:T(8,128)(2,1)}), bf16[1,256,640]{2,1,0:T(8,128)(2,1)}) %reduce-scatter.80.cloned.1.call-update) | async-done | bytes 327696 | tf_op jit(solution)/shard_map/reduce_scatter | solution.py:74
  1084.4 28.5 %all-gather.60.cloned.1.call-done = bf16[1,1024,640]{2,1,0:T(8,128)(2,1)} async-done(((bf16[1,256,640]{2,1,0:T(8,128)(2,1)}), bf16[1,1024,640]{2,1,0:T(8,128)(2,1)}) %all-gather.60.cloned.1.call-update) | async-done | bytes 1310736 | tf_op jit(solution)/shard_map/all_gather | solution.py:70
  1135.5 29.4 %reduce-scatter.82.cloned.1.call-done = bf16[1,256,640]{2,1,0:T(8,128)(2,1)} async-done(((bf16[1,1024,640]{2,1,0:T(8,128)(2,1)}), bf16[1,256,640]{2,1,0:T(8,128)(2,1)}) %reduce-scatter.82.cloned.1.call-update) | async-done | bytes 327696 | tf_op jit(solution)/shard_map/reduce_scatter | solution.py:74
  1173.7 28.7 %all-gather.62.cloned.1.call-done = bf16[1,1024,640]{2,1,0:T(8,128)(2,1)} async-done(((bf16[1,256,640]{2,1,0:T(8,128)(2,1)}), bf16[1,1024,640]{2,1,0:T(8,128)(2,1)}) %all-gather.62.cloned.1.call-update) | async-done | bytes 1310736 | tf_op jit(solution)/shard_map/all_gather | solution.py:70
  1211.5 29.4 %reduce-scatter.84.cloned.1.call-done = bf16[1,256,640]{2,1,0:T(8,128)(2,1)} async-done(((bf16[1,1024,640]{2,1,0:T(8,128)(2,1)}), bf16[1,256,640]{2,1,0:T(8,128)(2,1)}) %reduce-scatter.84.cloned.1.call-update) | async-done | bytes 327696 | tf_op jit(solution)/shard_map/reduce_scatter | solution.py:74
  1246.2 28.9 %all-gather.64.cloned.1.call-done = bf16[1,1024,640]{2,1,0:T(8,128)(2,1)} async-done(((bf16[1,256,640]{2,1,0:T(8,128)(2,1)}), bf16[1,1024,640]{2,1,0:T(8,128)(2,1)}) %all-gather.64.cloned.1.call-update) | async-done | bytes 1310736 | tf_op jit(solution)/shard_map/all_gather | solution.py:70
  1295.8 29.4 %reduce-scatter.86.cloned.1.call-done = bf16[1,256,640]{2,1,0:T(8,128)(2,1)} async-done(((bf16[1,1024,640]{2,1,0:T(8,128)(2,1)}), bf16[1,256,640]{2,1,0:T(8,128)(2,1)}) %reduce-scatter.86.cloned.1.call-update) | async-done | bytes 327696 | tf_op jit(solution)/shard_map/reduce_scatter | solution.py:74
  1334.1 28.5 %all-gather.66.cloned.1.call-done = bf16[1,1024,640]{2,1,0:T(8,128)(2,1)} async-done(((bf16[1,256,640]{2,1,0:T(8,128)(2,1)}), bf16[1,1024,640]{2,1,0:T(8,128)(2,1)}) %all-gather.66.cloned.1.call-update) | async-done | bytes 1310736 | tf_op jit(solution)/shard_map/all_gather | solution.py:70
  1371.6 29.4 %reduce-scatter.88.cloned.1.call-done = bf16[1,256,640]{2,1,0:T(8,128)(2,1)} async-done(((bf16[1,1024,640]{2,1,0:T(8,128)(2,1)}), bf16[1,256,640]{2,1,0:T(8,128)(2,1)}) %reduce-scatter.88.cloned.1.call-update) | async-done | bytes 327696 | tf_op jit(solution)/shard_map/reduce_scatter | solution.py:74
  1407.0 28.9 %all-gather.68.cloned.1.call-done = bf16[1,1024,640]{2,1,0:T(8,128)(2,1)} async-done(((bf16[1,256,640]{2,1,0:T(8,128)(2,1)}), bf16[1,1024,640]{2,1,0:T(8,128)(2,1)}) %all-gather.68.cloned.1.call-update) | async-done | bytes 1310736 | tf_op jit(solution)/shard_map/all_gather | solution.py:70
  1457.7 29.4 %reduce-scatter.90.cloned.1.call-done = bf16[1,256,640]{2,1,0:T(8,128)(2,1)} async-done(((bf16[1,1024,640]{2,1,0:T(8,128)(2,1)}), bf16[1,256,640]{2,1,0:T(8,128)(2,1)}) %reduce-scatter.90.cloned.1.call-update) | async-done | bytes 327696 | tf_op jit(solution)/shard_map/reduce_scatter | solution.py:74
  1495.5 28.7 %all-gather.70.cloned.1.call-done = bf16[1,1024,640]{2,1,0:T(8,128)(2,1)} async-done(((bf16[1,256,640]{2,1,0:T(8,128)(2,1)}), bf16[1,1024,640]{2,1,0:T(8,128)(2,1)}) %all-gather.70.cloned.1.call-update) | async-done | bytes 1310736 | tf_op jit(solution)/shard_map/all_gather | solution.py:70
  1533.3 29.4 %reduce-scatter.92.cloned.1.call-done = bf16[1,256,640]{2,1,0:T(8,128)(2,1)} async-done(((bf16[1,1024,640]{2,1,0:T(8,128)(2,1)}), bf16[1,256,640]{2,1,0:T(8,128)(2,1)}) %reduce-scatter.92.cloned.1.call-update) | async-done | bytes 327696 | tf_op jit(solution)/shard_map/reduce_scatter | solution.py:74
  1826.7 23.2 reduce-scatter.158.cloned.1.call-done
  1849.9 23.4 reduce-scatter.160.cloned.1.call-done
  1896.5 23.4 reduce-scatter.164.cloned.1.call-done
  1943.2 23.4 reduce-scatter.138.cloned.1.call-done
  1966.6 23.4 reduce-scatter.140.cloned.1.call-done
  1990.0 23.2 reduce-scatter.142.cloned.1.call-done
  2013.2 23.2 reduce-scatter.144.cloned.1.call-done
  2059.8 23.4 reduce-scatter.148.cloned.1.call-done
  2083.2 23.4 reduce-scatter.150.cloned.1.call-done
  2129.9 23.2 reduce-scatter.154.cloned.1.call-done
  2360.7 42.4 %all-reduce.92.cloned.1.call-done = (bf16[1,160,256]{2,1,0:T(8,128)(2,1)}, bf16[1,160,256]{2,1,0:T(8,128)(2,1)}) async-done(((bf16[1,160,256]{2,1,0:T(8,128)(2,1)}, bf16[1,160,256]{2,1,0:T(8,128)(2,1)}), (bf16[1,160,256]{2,1,0:T(8,128)(2,1)}, bf16[1,160,256]{2,1,0:T(8,128)(2,1)})) %all-reduce.92.cloned.1.call-update) | async-done | bytes 163856 | tf_op jit(solution)/shard_map/psum | solution.py:526
  2406.1 29.2 %reduce-scatter.94.cloned.1.call-done = bf16[1,256,640]{2,1,0:T(8,128)(2,1)} async-done(((bf16[1,1024,640]{2,1,0:T(8,128)(2,1)}), bf16[1,256,640]{2,1,0:T(8,128)(2,1)}) %reduce-scatter.94.cloned.1.call-update) | async-done | bytes 327696 | tf_op jit(solution)/shard_map/reduce_scatter | solution.py:74
  (1321 shorter events, 1104.8 us)
Async XLA Ops:
  7.2 83.2 %all-gather.34.cloned.1.call-start = ((), (), s32[]{:S(2)}) async-start(), calls=%async_computation.55 | async-start | bytes 1638400 | tf_op jit(solution)/shard_map/all_gather | solution.py:60
  32.2 100.8 %reduce-scatter.56.cloned.1.call-start = ((), (), s32[]{:S(2)}) async-start(), calls=%async_computation.56 | async-start | bytes 1638400 | tf_op jit(solution)/shard_map/reduce_scatter | solution.py:64
  104.7 86.1 %all-gather.36.cloned.1.call-start = ((), (), s32[]{:S(2)}) async-start(), calls=%async_computation.57 | async-start | bytes 1638400 | tf_op jit(solution)/shard_map/all_gather | solution.py:60
  138.0 89.8 %reduce-scatter.58.cloned.1.call-start = ((), (), s32[]{:S(2)}) async-start(), calls=%async_computation.58 | async-start | bytes 1638400 | tf_op jit(solution)/shard_map/reduce_scatter | solution.py:64
  388.0 73.7 %reduce-scatter.64.cloned.1.call-start = ((), (), s32[]{:S(2)}) async-start(), calls=%async_computation.64 | async-start | bytes 1638400 | tf_op jit(solution)/shard_map/reduce_scatter | solution.py:64
  541.4 73.7 %reduce-scatter.68.cloned.1.call-start = ((), (), s32[]{:S(2)}) async-start(), calls=%async_computation.68 | async-start | bytes 1638400 | tf_op jit(solution)/shard_map/reduce_scatter | solution.py:64
  694.7 74.1 %reduce-scatter.72.cloned.1.call-start = ((), (), s32[]{:S(2)}) async-start(), calls=%async_computation.72 | async-start | bytes 1638400 | tf_op jit(solution)/shard_map/reduce_scatter | solution.py:64
  920.6 80.8 %reduce-scatter.78.cloned.1.call-start = ((), (), s32[]{:S(2)}) async-start(), calls=%async_computation.78 | async-start | bytes 1638400 | tf_op jit(solution)/shard_map/reduce_scatter | solution.py:74
  1084.0 80.9 %reduce-scatter.82.cloned.1.call-start = ((), (), s32[]{:S(2)}) async-start(), calls=%async_computation.82 | async-start | bytes 1638400 | tf_op jit(solution)/shard_map/reduce_scatter | solution.py:74
  1246.2 79.1 %reduce-scatter.86.cloned.1.call-start = ((), (), s32[]{:S(2)}) async-start(), calls=%async_computation.86 | async-start | bytes 1638400 | tf_op jit(solution)/shard_map/reduce_scatter | solution.py:74
  1406.9 80.2 %reduce-scatter.90.cloned.1.call-start = ((), (), s32[]{:S(2)}) async-start(), calls=%async_computation.90 | async-start | bytes 1638400 | tf_op jit(solution)/shard_map/reduce_scatter | solution.py:74
  1567.5 148.7 %reduce-scatter.116.cloned.1.call-start = ((), (), s32[]{:S(2)}) async-start(), calls=%async_computation.105 | async-start | bytes 409600 | tf_op jit(solution)/shard_map/reduce_scatter | solution.py:123
  1570.4 145.8 %reduce-scatter.118.cloned.1.call-start = ((), (), s32[]{:S(2)}) async-start(), calls=%async_computation.106 | async-start | bytes 409600 | tf_op jit(solution)/shard_map/reduce_scatter | solution.py:123
  1573.1 143.0 %reduce-scatter.120.cloned.1.call-start = ((), (), s32[]{:S(2)}) async-start(), calls=%async_computation.107 | async-start | bytes 409600 | tf_op jit(solution)/shard_map/reduce_scatter | solution.py:123
  1575.6 140.6 %reduce-scatter.122.cloned.1.call-start = ((), (), s32[]{:S(2)}) async-start(), calls=%async_computation.108 | async-start | bytes 409600 | tf_op jit(solution)/shard_map/reduce_scatter | solution.py:123
  1578.6 137.6 %reduce-scatter.124.cloned.1.call-start = ((), (), s32[]{:S(2)}) async-start(), calls=%async_computation.109 | async-start | bytes 409600 | tf_op jit(solution)/shard_map/reduce_scatter | solution.py:123
  1603.3 118.5 %reduce-scatter.106.cloned.1.call-start = ((), (), s32[]{:S(2)}) async-start(), calls=%async_computation.100 | async-start | bytes 409600 | tf_op jit(solution)/shard_map/reduce_scatter | solution.py:120
  1606.1 136.2 %reduce-scatter.108.cloned.1.call-start = ((), (), s32[]{:S(2)}) async-start(), calls=%async_computation.101 | async-start | bytes 409600 | tf_op jit(solution)/shard_map/reduce_scatter | solution.py:120
  1608.9 153.9 %reduce-scatter.110.cloned.1.call-start = ((), (), s32[]{:S(2)}) async-start(), calls=%async_computation.102 | async-start | bytes 409600 | tf_op jit(solution)/shard_map/reduce_scatter | solution.py:120
  1611.7 171.6 %reduce-scatter.112.cloned.1.call-start = ((), (), s32[]{:S(2)}) async-start(), calls=%async_computation.103 | async-start | bytes 409600 | tf_op jit(solution)/shard_map/reduce_scatter | solution.py:120
  1614.5 189.3 %reduce-scatter.114.cloned.1.call-start = ((), (), s32[]{:S(2)}) async-start(), calls=%async_computation.104 | async-start | bytes 409600 | tf_op jit(solution)/shard_map/reduce_scatter | solution.py:120
  1626.8 199.9 %reduce-scatter.156.cloned.1.call-start = ((), (), s32[]{:S(2)}) async-start(), calls=%async_computation.125 | async-start | bytes 819200 | tf_op jit(solution)/shard_map/reduce_scatter | solution.py:135
  1630.3 219.6 %reduce-scatter.158.cloned.1.call-start = ((), (), s32[]{:S(2)}) async-start(), calls=%async_computation.126 | async-start | bytes 819200 | tf_op jit(solution)/shard_map/reduce_scatter | solution.py:135
  1633.8 239.5 %reduce-scatter.160.cloned.1.call-start = ((), (), s32[]{:S(2)}) async-start(), calls=%async_computation.127 | async-start | bytes 819200 | tf_op jit(solution)/shard_map/reduce_scatter | solution.py:135
  1637.2 259.3 %reduce-scatter.162.cloned.1.call-start = ((), (), s32[]{:S(2)}) async-start(), calls=%async_computation.128 | async-start | bytes 819200 | tf_op jit(solution)/shard_map/reduce_scatter | solution.py:135
  1640.7 279.1 %reduce-scatter.164.cloned.1.call-start = ((), (), s32[]{:S(2)}) async-start(), calls=%async_computation.129 | async-start | bytes 819200 | tf_op jit(solution)/shard_map/reduce_scatter | solution.py:135
  1644.1 299.0 %reduce-scatter.136.cloned.1.call-start = ((), (), s32[]{:S(2)}) async-start(), calls=%async_computation.115 | async-start | bytes 819200 | tf_op jit(solution)/shard_map/reduce_scatter | solution.py:129
  1647.6 319.0 %reduce-scatter.138.cloned.1.call-start = ((), (), s32[]{:S(2)}) async-start(), calls=%async_computation.116 | async-start | bytes 819200 | tf_op jit(solution)/shard_map/reduce_scatter | solution.py:129
  1651.0 339.0 %reduce-scatter.140.cloned.1.call-start = ((), (), s32[]{:S(2)}) async-start(), calls=%async_computation.117 | async-start | bytes 819200 | tf_op jit(solution)/shard_map/reduce_scatter | solution.py:129
  1654.4 358.8 %reduce-scatter.142.cloned.1.call-start = ((), (), s32[]{:S(2)}) async-start(), calls=%async_computation.118 | async-start | bytes 819200 | tf_op jit(solution)/shard_map/reduce_scatter | solution.py:129
  1658.2 378.3 %reduce-scatter.144.cloned.1.call-start = ((), (), s32[]{:S(2)}) async-start(), calls=%async_computation.119 | async-start | bytes 819200 | tf_op jit(solution)/shard_map/reduce_scatter | solution.py:129
  1661.6 398.2 %reduce-scatter.146.cloned.1.call-start = ((), (), s32[]{:S(2)}) async-start(), calls=%async_computation.120 | async-start | bytes 819200 | tf_op jit(solution)/shard_map/reduce_scatter | solution.py:132
  1665.0 418.2 %reduce-scatter.148.cloned.1.call-start = ((), (), s32[]{:S(2)}) async-start(), calls=%async_computation.121 | async-start | bytes 819200 | tf_op jit(solution)/shard_map/reduce_scatter | solution.py:132
  1668.5 438.1 %reduce-scatter.150.cloned.1.call-start = ((), (), s32[]{:S(2)}) async-start(), calls=%async_computation.122 | async-start | bytes 819200 | tf_op jit(solution)/shard_map/reduce_scatter | solution.py:132
  1671.9 457.9 %reduce-scatter.152.cloned.1.call-start = ((), (), s32[]{:S(2)}) async-start(), calls=%async_computation.123 | async-start | bytes 819200 | tf_op jit(solution)/shard_map/reduce_scatter | solution.py:132
  1675.4 477.7 %reduce-scatter.154.cloned.1.call-start = ((), (), s32[]{:S(2)}) async-start(), calls=%async_computation.124 | async-start | bytes 819200 | tf_op jit(solution)/shard_map/reduce_scatter | solution.py:132
  1678.8 495.5 %reduce-scatter.126.cloned.1.call-start = ((), (), s32[]{:S(2)}) async-start(), calls=%async_computation.110 | async-start | bytes 409600 | tf_op jit(solution)/shard_map/reduce_scatter | solution.py:126
  1681.7 513.1 %reduce-scatter.128.cloned.1.call-start = ((), (), s32[]{:S(2)}) async-start(), calls=%async_computation.111 | async-start | bytes 409600 | tf_op jit(solution)/shard_map/reduce_scatter | solution.py:126
  1684.5 530.8 %reduce-scatter.130.cloned.1.call-start = ((), (), s32[]{:S(2)}) async-start(), calls=%async_computation.112 | async-start | bytes 409600 | tf_op jit(solution)/shard_map/reduce_scatter | solution.py:126
  1687.3 548.6 %reduce-scatter.132.cloned.1.call-start = ((), (), s32[]{:S(2)}) async-start(), calls=%async_computation.113 | async-start | bytes 409600 | tf_op jit(solution)/shard_map/reduce_scatter | solution.py:126
  1690.2 566.3 %reduce-scatter.134.cloned.1.call-start = ((), (), s32[]{:S(2)}) async-start(), calls=%async_computation.114 | async-start | bytes 409600 | tf_op jit(solution)/shard_map/reduce_scatter | solution.py:126
  1693.0 583.9 %reduce-scatter.96.cloned.1.call-start = ((), (), s32[]{:S(2)}) async-start(), calls=%async_computation.95 | async-start | bytes 409600 | tf_op jit(solution)/shard_map/reduce_scatter | solution.py:117
  1695.7 601.7 %reduce-scatter.98.cloned.1.call-start = ((), (), s32[]{:S(2)}) async-start(), calls=%async_computation.96 | async-start | bytes 409600 | tf_op jit(solution)/shard_map/reduce_scatter | solution.py:117
  1698.5 619.5 %reduce-scatter.100.cloned.1.call-start = ((), (), s32[]{:S(2)}) async-start(), calls=%async_computation.97 | async-start | bytes 409600 | tf_op jit(solution)/shard_map/reduce_scatter | solution.py:117
  1701.3 637.0 %reduce-scatter.102.cloned.1.call-start = ((), (), s32[]{:S(2)}) async-start(), calls=%async_computation.98 | async-start | bytes 409600 | tf_op jit(solution)/shard_map/reduce_scatter | solution.py:117
  1704.0 654.9 %reduce-scatter.104.cloned.1.call-start = ((), (), s32[]{:S(2)}) async-start(), calls=%async_computation.99 | async-start | bytes 409600 | tf_op jit(solution)/shard_map/reduce_scatter | solution.py:117
  1714.0 689.0 %all-reduce.92.cloned.1.call-start = ((), (), s32[]{:S(2)}) async-start(), calls=%async_computation.130 | async-start | bytes 327680 | tf_op jit(solution)/shard_map/psum | solution.py:526
  1805.7 629.7 %reduce-scatter.94.cloned.1.call-start = ((), (), s32[]{:S(2)}) async-start(), calls=%async_computation.94 | async-start | bytes 1638400 | tf_op jit(solution)/shard_map/reduce_scatter | solution.py:74
  (370 other events, 14915.1 us)
Sparse Core Ops, SparseCore 0:
  32.3 27.0 all-gather.33
  104.8 28.0 reduce-scatter.55
  138.1 28.7 all-gather.35
  199.1 28.6 reduce-scatter.57
  235.5 28.8 all-gather.37
  278.7 29.3 reduce-scatter.59
  313.3 28.7 all-gather.39
  350.4 29.3 reduce-scatter.61
  388.2 28.8 all-gather.41
  432.4 29.3 reduce-scatter.63
  466.3 28.7 all-gather.43
  503.6 29.3 reduce-scatter.65
  541.5 28.8 all-gather.45
  585.7 29.2 reduce-scatter.67
  619.6 28.7 all-gather.47
  656.9 29.3 reduce-scatter.69
  694.8 28.7 all-gather.49
  739.4 29.3 reduce-scatter.71
  774.4 28.7 all-gather.51
  811.8 29.3 reduce-scatter.73
  846.4 28.7 all-gather.53
  884.3 29.3 reduce-scatter.75
  920.8 28.7 all-gather.55
  972.1 29.2 reduce-scatter.77
  1010.3 28.7 all-gather.57
  1048.2 29.3 reduce-scatter.79
  1084.1 28.7 all-gather.59
  1135.5 29.2 reduce-scatter.81
  1173.6 28.7 all-gather.61
  1211.5 29.3 reduce-scatter.83
  1246.3 28.7 all-gather.63
  1295.9 29.3 reduce-scatter.85
  1333.8 28.7 all-gather.65
  1371.7 29.3 reduce-scatter.87
  1407.0 28.7 all-gather.67
  1457.7 29.2 reduce-scatter.89
  1495.4 28.7 all-gather.69
  1533.3 29.3 reduce-scatter.91
  1567.6 28.7 all-gather.71
  1828.8 21.0 reduce-scatter.157
  1945.5 21.0 reduce-scatter.137
  1968.9 21.0 reduce-scatter.139
  1992.1 21.0 reduce-scatter.141
  2015.3 21.0 reduce-scatter.143
  2108.8 21.0 reduce-scatter.151
  2132.0 21.0 reduce-scatter.153
  2362.4 40.6 all-reduce.91
  2406.1 29.2 reduce-scatter.93
  (28 shorter events, 534.9 us)
where the time goes:
time: 2490 us; the launch traced here: 2480 us
  waiting for transfers between devices  1770 us (71%)
  matrix products  271 us (11%)
  other arithmetic  200 us (8%)
  blocking collectives  153 us (6%)
  local copies, waits for them, and re-layouts  39.8 us (2%)
    reduce_scatter x10, waiting for transfers between devices, fold_grads(): lax.psum_scatter(partial_rows.astype(jnp.bfloat16), 'tensor', scatter_dim...  294 us
    reduce_scatter x10, waiting for transfers between devices, fold_rows(): lax.psum_scatter(partial_rows.astype(jnp.bfloat16), 'tensor', scatter_dim...  292 us
    all_gather x10, waiting for transfers between devices, spread_grads(): return lax.all_gather(local_rows, 'tensor', axis=1, tiled=True)  277 us
    all_gather x10, waiting for transfers between devices, spread_rows(): return lax.all_gather(local_rows, 'tensor', axis=1, tiled=True)  230 us
    reduce_scatter x5, waiting for transfers between devices, reduce_weights(): lax.psum_scatter(grads_full[11].astype(jnp.bfloat16), 'dp', scatter_dimen...  115 us
    reduce_scatter x5, waiting for transfers between devices, reduce_weights(): lax.psum_scatter(grads_full[10].astype(jnp.bfloat16), 'dp', scatter_dimen...  114 us
    reduce_scatter x5, waiting for transfers between devices, reduce_weights(): lax.psum_scatter(grads_full[12].astype(jnp.bfloat16), 'dp', scatter_dimen...  107 us
    reduce_scatter x5, waiting for transfers between devices, reduce_weights(): lax.psum_scatter(grads_full[9].astype(jnp.bfloat16), 'dp', scatter_dimens...  101 us
  transfers between devices with their start and end apart: 84, of which 77 were waited for; matrix products, arithmetic and copies ran while one was open for 6% of the time, Pallas kernels for 0%

commit v1 on v0

v1 whole, which is shorter than its diff:
```python
from functools import partial
import math

import jax
import jax.numpy as jnp
from jax import lax
from jax.sharding import PartitionSpec as P

WIN = 512


EPSILON = 1e-06
NEGATIVE = -1e30


def norm_gain(values, scales):
    return values * lax.rsqrt(jnp.mean(values * values, axis=-1, keepdims=True) + EPSILON) * scales


def rotate(values, cosine_table, sine_table):
    halved = values.shape[-1] // 2
    former = values[..., :halved]
    latter = values[..., halved:]
    return jnp.concatenate(
        [former * cosine_table - latter * sine_table, latter * cosine_table + former * sine_table],
        axis=-1,
    )


def query_path(raw_values, scales, cosine_table, sine_table):
    return rotate(norm_gain(raw_values, scales), cosine_table, sine_table) * raw_values.shape[
        -1
    ] ** (-0.5)


def key_path(raw_values, scales, cosine_table, sine_table):
    return rotate(norm_gain(raw_values, scales), cosine_table, sine_table)


def gated_unit(gate_proj, projected_up):
    return jax.nn.gelu(gate_proj, approximate=True) * projected_up


def cross(block):
    return lax.ppermute(block, "section", [(0, 1), (1, 0)])


def half_swap(mine, pair_rows):
    core = lax.axis_index("section")
    keep = lax.dynamic_slice_in_dim(mine, core * pair_rows, pair_rows, axis=0)
    give = lax.dynamic_slice_in_dim(mine, (1 - core) * pair_rows, pair_rows, axis=0)
    got = cross(give)
    first = core == 0
    return jnp.where(first, keep, got), jnp.where(first, got, keep)


def gather_all(shard):
    return lax.all_gather(shard, ("tensor", "dp", "section"), axis=0, tiled=True)


def dot(spec, left, right):
    return jnp.einsum(spec, left, right, preferred_element_type=jnp.float32)


def score_parts(tensor_size, span):
    half = span // 2
    reach = -(-WIN // span)
    parts = []
    step = max(1, min(tensor_size, reach))
    for begin in range(0, tensor_size, step):
        end = min(begin + step, tensor_size)
        parts.append((begin * half, end * half, max(0, begin - reach) * span, end * span))
    return parts


def masked_scores(queries, keys, row_pos, part):
    r0, r1, k0, k1 = part
    scores = dot("hqd,kd->hqk", queries[:, r0:r1], keys[k0:k1])
    distance = row_pos[r0:r1, None] - jnp.arange(k0, k1, dtype=jnp.int32)[None, :]
    return jnp.where((distance >= 0) & (distance < WIN), scores, NEGATIVE)


def natural_order(mine, tensor_size):
    other = cross(mine)
    first = lax.axis_index("section") == 0
    width = mine.shape[-1]
    pair = jnp.stack(
        [
            jnp.where(first, mine, other).reshape(tensor_size, -1, width),
            jnp.where(first, other, mine).reshape(tensor_size, -1, width),
        ],
        axis=1,
    )
    return pair.reshape(-1, width)


def sum_own(whole, tensor_size):
    core = lax.axis_index("section")
    width = whole.shape[-1]
    split = whole.reshape(tensor_size, 2, -1, width)
    own = lax.dynamic_index_in_dim(split, core, axis=1, keepdims=False)
    give = lax.dynamic_index_in_dim(split, 1 - core, axis=1, keepdims=False)
    got = cross(give.astype(jnp.bfloat16)).astype(jnp.float32)
    return (own + got).reshape(-1, width)


def forward_attention(u, weights, gains, row_pos, tables, tensor_size, span):
    pre_attn, post_attn, pre_ffn, post_ffn, query_scale, key_scale = gains
    wq, wo, wkv = weights
    cos_rows, sin_rows = tables
    head = wq.shape[2]
    normed = norm_gain(u, pre_attn).astype(jnp.bfloat16)
    kv_raw = dot("mv,vn->mn", normed, wkv)
    key_raw, values = kv_raw[:, :head], kv_raw[:, head:].astype(jnp.bfloat16)
    keys = key_path(key_raw, key_scale, cos_rows, sin_rows).astype(jnp.bfloat16)
    kv_all = natural_order(jnp.concatenate([keys, values], axis=-1), tensor_size)
    keys_all, values_all = kv_all[:, :head], kv_all[:, head:]
    query_raw = dot("mv,tvn->tmn", normed, wq)
    queries = query_path(query_raw, query_scale, cos_rows, sin_rows).astype(jnp.bfloat16)
    outs, totals = [], []
    for part in score_parts(tensor_size, span):
        scores = masked_scores(queries, keys_all, row_pos, part)
        highest = jnp.max(scores, axis=-1, keepdims=True)
        log_total = highest + jnp.log(jnp.sum(jnp.exp(scores - highest), axis=-1, keepdims=True))
        probs = jnp.exp(scores - log_total).astype(jnp.bfloat16)
        outs.append(dot("hqk,kd->hqd", probs, values_all[part[2] : part[3]]).astype(jnp.bfloat16))
        totals.append(log_total)
    attended = jnp.concatenate(outs, axis=1)
    branch = dot("tmn,tvn->mv", attended, wo)
    hidden = u + norm_gain(branch, post_attn)
    kept = (u, normed, query_raw, key_raw, queries, keys_all, values_all, totals, attended, branch)
    return hidden, kept


def forward_ffn(hidden, weights, gains):
    pre_ffn, post_ffn = gains[2], gains[3]
    wg, wu, wd = weights
    ffn_input = norm_gain(hidden, pre_ffn).astype(jnp.bfloat16)
    gate_proj = dot("mv,tvn->tmn", ffn_input, wg)
    up_proj = dot("mv,tvn->tmn", ffn_input, wu)
    product = gated_unit(gate_proj, up_proj).astype(jnp.bfloat16)
    ffn_output = dot("tmn,tvn->mv", product, wd)
    result = hidden + norm_gain(ffn_output, post_ffn)
    return result, (hidden, ffn_input, gate_proj, up_proj, product, ffn_output)


def backward_ffn(grad_output, kept, weights, gains):
    pre_ffn, post_ffn = gains[2], gains[3]
    wg, wu, wd = weights
    hidden, ffn_input, gate_proj, up_proj, product, ffn_output = kept
    output_grad, post_ffn_grad = jax.vjp(norm_gain, ffn_output, post_ffn)[1](grad_output)
    output_grad = output_grad.astype(jnp.bfloat16)
    product_grad = dot("mv,tvn->tmn", output_grad, wd)
    down_grad = dot("mv,tmn->tvn", output_grad, product).astype(jnp.bfloat16)
    gate_grad, up_grad = jax.vjp(gated_unit, gate_proj, up_proj)[1](product_grad)
    gate_grad = gate_grad.astype(jnp.bfloat16)
    up_grad = up_grad.astype(jnp.bfloat16)
    ffn_input_grad = dot("tmn,tvn->mv", gate_grad, wg) + dot("tmn,tvn->mv", up_grad, wu)
    gate_weight_grad = dot("mv,tmn->tvn", ffn_input, gate_grad).astype(jnp.bfloat16)
    up_weight_grad = dot("mv,tmn->tvn", ffn_input, up_grad).astype(jnp.bfloat16)
    hidden_part, pre_ffn_grad = jax.vjp(norm_gain, hidden, pre_ffn)[1](ffn_input_grad)
    hidden_grad = grad_output + hidden_part
    packed = jnp.concatenate([gate_weight_grad, up_weight_grad, down_grad], axis=-1)
    return hidden_grad, packed, (pre_ffn_grad, post_ffn_grad)


def backward_attention(hidden_grad, kept, weights, gains, row_pos, tables, tensor_size, span):
    pre_attn, post_attn, pre_ffn, post_ffn, query_scale, key_scale = gains
    wq, wo, wkv = weights
    cos_rows, sin_rows = tables
    u, normed, query_raw, key_raw, queries, keys_all, values_all, totals, attended, branch = kept
    head = wq.shape[2]
    length = keys_all.shape[0]
    branch_grad, post_attn_grad = jax.vjp(norm_gain, branch, post_attn)[1](hidden_grad)
    branch_grad = branch_grad.astype(jnp.bfloat16)
    attended_grad = dot("mv,tvn->tmn", branch_grad, wo).astype(jnp.bfloat16)
    out_grad = dot("mv,tmn->tvn", branch_grad, attended).astype(jnp.bfloat16)
    query_grads = []
    kv_sum = jnp.zeros((length, 2 * head), jnp.float32)
    for part, log_total in zip(score_parts(tensor_size, span), totals):
        r0, r1, k0, k1 = part
        weights_exact = jnp.exp(masked_scores(queries, keys_all, row_pos, part) - log_total)
        out_block = attended_grad[:, r0:r1]
        probs_grad = dot("hqd,kd->hqk", out_block, values_all[k0:k1])
        inner = jnp.sum(weights_exact * probs_grad, axis=-1, keepdims=True)
        score_grad = (weights_exact * (probs_grad - inner)).astype(jnp.bfloat16)
        query_grads.append(dot("hqk,kd->hqd", score_grad, keys_all[k0:k1]))
        key_term = dot("hqk,hqd->kd", score_grad, queries[:, r0:r1])
        value_term = dot("hqk,hqd->kd", weights_exact.astype(jnp.bfloat16), out_block)
        kv_term = jnp.concatenate([key_term, value_term], axis=-1)
        kv_sum = kv_sum + jnp.pad(kv_term, ((k0, length - k1), (0, 0)))
    kv_own = sum_own(kv_sum, tensor_size)
    query_grad = jnp.concatenate(query_grads, axis=1)
    value_grad = kv_own[:, head:].astype(jnp.bfloat16)
    raw_query_grad, query_scale_grad = jax.vjp(
        partial(query_path, cosine_table=cos_rows, sine_table=sin_rows), query_raw, query_scale
    )[1](query_grad)
    raw_query_grad = raw_query_grad.astype(jnp.bfloat16)
    raw_key_grad, key_scale_grad = jax.vjp(
        partial(key_path, cosine_table=cos_rows, sine_table=sin_rows), key_raw, key_scale
    )[1](kv_own[:, :head])
    raw_kv_grad = jnp.concatenate([raw_key_grad.astype(jnp.bfloat16), value_grad], axis=-1)
    normed_grad = dot("tmn,tvn->mv", raw_query_grad, wq) + dot("mn,vn->mv", raw_kv_grad, wkv)
    query_weight_grad = dot("mv,tmn->tvn", normed, raw_query_grad).astype(jnp.bfloat16)
    kv_weight_grad = dot("mv,mn->vn", normed, raw_kv_grad).astype(jnp.bfloat16)
    input_part, pre_attn_grad = jax.vjp(norm_gain, u, pre_attn)[1](normed_grad)
    u_grad = hidden_grad + input_part
    return (
        u_grad,
        (query_weight_grad, out_grad, kv_weight_grad),
        (pre_attn_grad, post_attn_grad, query_scale_grad, key_scale_grad),
    )


def reduce_packed(packed, rows):
    tensor_size, _, width = packed.shape
    core = lax.axis_index("section")
    split = packed.reshape(tensor_size, -1, 2, rows // 2, width)
    own = lax.dynamic_index_in_dim(split, core, axis=2, keepdims=False)
    give = lax.dynamic_index_in_dim(split, 1 - core, axis=2, keepdims=False)
    total = own.astype(jnp.float32) + cross(give).astype(jnp.float32)
    total = total.astype(jnp.bfloat16).reshape(-1, width)
    total = lax.psum_scatter(total, "tensor", scatter_dimension=0, tiled=True)
    return lax.psum_scatter(total, "dp", scatter_dimension=0, tiled=True)


def own_layer(halves):
    first = lax.axis_index("section") == 0
    keep = jnp.where(first, halves[0], halves[1])
    got = cross(jnp.where(first, halves[1], halves[0]))
    return jnp.concatenate(
        [jnp.where(first, keep, got), jnp.where(first, got, keep)], axis=0
    ).astype(jnp.float32)


def local(
    inputs,
    cotangent,
    pre_attn_gain,
    post_attn_gain,
    pre_ffn_gain,
    post_ffn_gain,
    query_gain,
    key_gain,
    query_weight,
    key_weight,
    value_weight,
    out_weight,
    gate_weight,
    up_weight,
    down_weight,
):
    tensor_size = lax.axis_size("tensor")
    dp_size = lax.axis_size("dp")
    core = lax.axis_index("section")
    micro_count, _, span, width = inputs.shape
    half = span // 2
    rows, head = query_weight.shape[1:]
    hidden_cols = gate_weight.shape[2]
    depth = rows * dp_size

    def to_chip(block):
        own = lax.dynamic_slice_in_dim(block[:, 0], core * half, half, axis=1)
        moved = lax.all_to_all(own, "tensor", split_axis=0, concat_axis=0, tiled=True)
        return moved.reshape(-1, width)

    def from_chip(first_layer, second_layer):
        both = jnp.stack([first_layer, second_layer]).reshape(2 * tensor_size, half, width)
        moved = lax.all_to_all(both, ("section", "tensor"), split_axis=0, concat_axis=0, tiled=True)
        moved = moved.reshape(2, tensor_size, half, width).transpose(1, 0, 2, 3)
        return moved.reshape(1, tensor_size, 1, span, width)

    gain_parts = (pre_attn_gain, post_attn_gain, pre_ffn_gain, post_ffn_gain, query_gain, key_gain)
    gain_sizes = [part.shape[1] for part in gain_parts]
    gain_row = jnp.concatenate([part[0] for part in gain_parts])
    gain_all = lax.all_gather(gain_row, ("section", "dp"), axis=0, tiled=True)
    gain_all = gain_all.reshape(2, dp_size, -1).astype(jnp.float32)
    gains = []
    for index in range(2):
        pieces, at = [], 0
        for size in gain_sizes:
            pieces.append(gain_all[index, :, at : at + size].reshape(-1))
            at += size
        gains.append(tuple(pieces))

    quarter = rows // tensor_size
    kv_rows = jnp.concatenate([key_weight[0], value_weight[0]], axis=-1)
    kv_rows = lax.dynamic_slice_in_dim(
        kv_rows, lax.axis_index("tensor") * quarter, quarter, axis=0
    ).reshape(rows, -1)
    attention_shard = jnp.concatenate([query_weight[0], out_weight[0].T, kv_rows], axis=-1)
    ffn_shard = jnp.concatenate([gate_weight[0], up_weight[0], down_weight[0].T], axis=-1)
    attention_shards = half_swap(attention_shard, rows // 2)
    ffn_shards = half_swap(ffn_shard, rows // 2)

    def attention_weights(index):
        whole = gather_all(attention_shards[index]).reshape(tensor_size, depth, -1)
        wkv = whole[:, :, 2 * head :].reshape(tensor_size, dp_size, quarter, 2 * head)
        wkv = wkv.transpose(1, 0, 2, 3).reshape(depth, 2 * head)
        return whole[:, :, :head], whole[:, :, head : 2 * head], wkv

    def ffn_weights(index):
        whole = gather_all(ffn_shards[index]).reshape(tensor_size, depth, -1)
        return tuple(
            whole[:, :, n * hidden_cols : (n + 1) * hidden_cols] for n in range(3)
        )

    stream = to_chip(inputs).astype(jnp.float32)
    attention = [attention_weights(0), None]
    ffn = [ffn_weights(0), None]
    attention[1] = attention_weights(1)
    ffn[1] = ffn_weights(1)
    length = span * tensor_size
    row = jnp.arange(tensor_size * half, dtype=jnp.int32)
    row_pos = (row // half) * span + core * half + row % half
    halved = head // 2
    indices = jnp.arange(halved, dtype=jnp.int32).astype(jnp.float32)
    inverse = jnp.exp(indices * (-2.0 * math.log(10000.0) / head))
    angles = row_pos.astype(jnp.float32)[:, None] * inverse[None, :]
    tables = (jnp.cos(angles), jnp.sin(angles))

    kept_attention, kept_ffn, rounded = [], [], []
    for index in range(2):
        hidden, kept = forward_attention(
            stream, attention[index], gains[index], row_pos, tables, tensor_size, span
        )
        kept_attention.append(kept)
        result, kept = forward_ffn(hidden, ffn[index], gains[index])
        kept_ffn.append(kept)
        rounded.append(result.astype(jnp.bfloat16))
        stream = rounded[-1].astype(jnp.float32)
    layer_outputs = from_chip(rounded[0], rounded[1])

    grad = to_chip(cotangent).astype(jnp.float32)
    attention_sums, ffn_sums, input_grads = [None, None], [None, None], [None, None]
    for index in (1, 0):
        grad, packed, ffn_gain_grads = backward_ffn(
            grad, kept_ffn[index], ffn[index], gains[index]
        )
        ffn_sums[index] = reduce_packed(packed, rows)
        grad, matrix_grads, gain_grads = backward_attention(
            grad,
            kept_attention[index],
            attention[index],
            gains[index],
            row_pos,
            tables,
            tensor_size,
            span,
        )
        gain_list = gain_grads[:2] + ffn_gain_grads + gain_grads[2:]
        gain_block = jnp.concatenate([part.reshape(dp_size, -1) for part in gain_list], axis=1)
        count = gain_block.shape[1]
        lanes = max(128, -(-count // rows))
        gain_block = jnp.pad(gain_block, ((0, 0), (0, rows * lanes - count)))
        gain_block = gain_block.reshape(depth, lanes).astype(jnp.bfloat16)
        shared = jnp.concatenate([matrix_grads[2], gain_block], axis=-1)
        shared = jnp.broadcast_to(shared[None], (tensor_size,) + shared.shape)
        packed = jnp.concatenate([matrix_grads[0], matrix_grads[1], shared], axis=-1)
        attention_sums[index] = reduce_packed(packed, rows)
        rounded_grad = grad.astype(jnp.bfloat16)
        input_grads[index] = rounded_grad
        grad = rounded_grad.astype(jnp.float32)

    input_grad = from_chip(input_grads[0], input_grads[1]).astype(jnp.float32)
    ffn_total = own_layer(ffn_sums)
    attention_total = own_layer(attention_sums)
    gain_total = attention_total[:, 4 * head :].reshape(-1)
    gain_outs, at = [], 0
    for size in gain_sizes:
        gain_outs.append(gain_total[at : at + size])
        at += size
    finished = tuple(gain_outs) + (
        attention_total[:, :head],
        attention_total[:, 2 * head : 3 * head],
        attention_total[:, 3 * head : 4 * head],
        attention_total[:, head : 2 * head].T,
        ffn_total[:, :hidden_cols],
        ffn_total[:, hidden_cols : 2 * hidden_cols],
        ffn_total[:, 2 * hidden_cols :].T,
    )
    return (layer_outputs, input_grad) + tuple(part[None] for part in finished)


def solution(mesh):
    return jax.shard_map(
        local,
        mesh=mesh,
        in_specs=(
            P(None, "dp", "tensor", None),
            P(None, "dp", "tensor", None),
            P("section", "dp"),
            P("section", "dp"),
            P("section", "dp"),
            P("section", "dp"),
            P("section", "dp"),
            P("section", "dp"),
            P("section", "dp", "tensor"),
            P("section", "dp", None),
            P("section", "dp", None),
            P("section", "tensor", "dp"),
            P("section", "dp", "tensor"),
            P("section", "dp", "tensor"),
            P("section", "tensor", "dp"),
        ),
        out_specs=(
            P("section", None, "dp", "tensor", None),
            P("section", None, "dp", "tensor", None),
            P("section", "dp"),
            P("section", "dp"),
            P("section", "dp"),
            P("section", "dp"),
            P("section", "dp"),
            P("section", "dp"),
            P("section", "dp", "tensor"),
            P("section", "dp", None),
            P("section", "dp", None),
            P("section", "tensor", "dp"),
            P("section", "dp", "tensor"),
            P("section", "dp", "tensor"),
            P("section", "tensor", "dp"),
        ),
        check_vma=False,
    )
```

time: 2490 us -> 814 us (0.33)
  waiting for transfers between devices: 1770 us -> 395 us
  matrix products: 271 us -> 141 us
  blocking collectives: 153 us -> 23.6 us
  other arithmetic: 200 us -> 94.1 us
  local copies, waits for them, and re-layouts: 39.8 us -> 113 us
    reduce_scatter x55 -> x8, waiting for transfers between devices: 1210 us -> 187 us  [the longest x4 98.2 us: reduce_packed(): return lax.psum_scatter(total, 'dp', scatter_dimension=0, tiled=True)]
    all_gather x20 -> x4, waiting for transfers between devices: 507 us -> 166 us  [gather_all(): lax.all_gather(shard, ('tensor', 'dp', 'section'), axis=0, tiled=True)]
    dot_general x165 -> x60, matrix products: 271 us -> 141 us  [dot(): return jnp.einsum(spec, left, right, preferred_element_type=jnp.float32)]
    all_gather x7 -> x1, blocking collectives: 110 us -> 23.6 us  [local(): gain_all = lax.all_gather(gain_row, ('section', 'dp'), axis=0, tiled=True)]
    psum x1 -> x0, waiting for transfers between devices: 42.4 us -> none  [local(): lax.psum(summed[7].astype(jnp.bfloat16), 'tensor').astype(jnp.float32)]
    unnamed x2 -> x0, blocking collectives: 33.5 us -> none
    all_to_all x0 -> x4, waiting for transfers between devices: none -> 25.2 us  [the longest x2 25.2 us: from_chip(): lax.all_to_all(both, ('section', 'tensor'), split_axis=0, concat_axis=0,...]
  transfers between devices with their start and end apart: 84 -> 28, of which waited for: 77 -> 15; matrix products, arithmetic and copies ran while one was open for 6% -> 26% of each run, Pallas kernels for 0% -> 0%
where the time goes in v1:
time: 814 us; the launch traced here: 806 us
  waiting for transfers between devices  395 us (49%)
  matrix products  141 us (17%)
  local copies, waits for them, and re-layouts  113 us (14%)
  other arithmetic  94.1 us (12%)
  blocking collectives  23.6 us (3%)
  starting transfers between devices  21.5 us (3%)
  between operations  17.6 us (2%)
    all_gather x4, waiting for transfers between devices, gather_all(): lax.all_gather(shard, ('tensor', 'dp', 'section'), axis=0, tiled=True)  166 us
    dot_general x60, matrix products, dot(): return jnp.einsum(spec, left, right, preferred_element_type=jnp.float32)  141 us
    reduce_scatter x4, waiting for transfers between devices, reduce_packed(): return lax.psum_scatter(total, 'dp', scatter_dimension=0, tiled=True)  98.2 us
    reduce_scatter x4, waiting for transfers between devices, reduce_packed(): total = lax.psum_scatter(total, 'tensor', scatter_dimension=0, tiled=True)  89 us
    unnamed x449, local copies, waits for them, and re-layouts  27.3 us
    all_to_all x2, waiting for transfers between devices, from_chip(): lax.all_to_all(both, ('section', 'tensor'), split_axis=0, concat_axis=0,...  25.2 us
    all_gather x1, blocking collectives, local(): gain_all = lax.all_gather(gain_row, ('section', 'dp'), axis=0, tiled=True)  23.6 us
    concatenate x2, local copies, waits for them, and re-layouts, backward_ffn(): jnp.concatenate([gate_weight_grad, up_weight_grad, down_grad], axis=-1)  21.4 us
  transfers between devices with their start and end apart: 28, of which 15 were waited for; matrix products, arithmetic and copies ran while one was open for 26% of the time, Pallas kernels for 0%

profile of v1, /device:TPU:0, one launch (start us, length us, event | category | flops | bytes accessed | tf_op | source)
XLA Modules:
  0.0 805.6 jit_solution(1999014625945279816)
XLA Ops:
  16.7 5.1 all-to-all-start
  22.1 23.6 %all-gather = bf16[8,1,768]{2,1,0:T(2,128)(2,1)S(1)} all-gather(bf16[1,1,768]{2,1,0:T(2,128)(2,1)S(1)} %reshape.654), channel_id=1, replica_groups=mesh['section'=2,'dp'=4,'tensor'=4] {'section','dp'}, dimensions={0}, use_global_device_ids=true | all-gather | bytes 13824 | tf_op jit(solution)/shard_map/all_gather | solution.py:276
  53.5 4.3 all-to-all-start.2
  59.4 23.0 %all-gather.6.cloned.1.call-done = bf16[2560,640]{1,0:T(8,128)(2,1)} async-done(((bf16[80,640]{1,0:T(8,128)(2,1)}), bf16[2560,640]{1,0:T(8,128)(2,1)}) %all-gather.6.cloned.1.call-update) | async-done | bytes 3276816 | tf_op jit(solution)/shard_map/all_gather | solution.py:58
  93.2 50.4 %all-gather.10.cloned.1.call-done = bf16[2560,640]{1,0:T(8,128)(2,1)} async-done(((bf16[80,640]{1,0:T(8,128)(2,1)}), bf16[2560,640]{1,0:T(8,128)(2,1)}) %all-gather.10.cloned.1.call-update) | async-done | bytes 3276816 | tf_op jit(solution)/shard_map/all_gather | solution.py:58
  165.1 56.0 %all-gather.8.cloned.1.call-done = bf16[2560,1536]{1,0:T(8,128)(2,1)} async-done(((bf16[80,1536]{1,0:T(8,128)(2,1)}), bf16[2560,1536]{1,0:T(8,128)(2,1)}) %all-gather.8.cloned.1.call-update) | async-done | bytes 7864336 | tf_op jit(solution)/shard_map/all_gather | solution.py:58
  221.1 3.7 fusion.48
  225.1 4.6 fusion.23
  244.5 2.8 pad_maximum_fusion.8
  262.2 36.3 %all-gather.12.cloned.1.call-done = bf16[2560,1536]{1,0:T(8,128)(2,1)} async-done(((bf16[80,1536]{1,0:T(8,128)(2,1)}), bf16[2560,1536]{1,0:T(8,128)(2,1)}) %all-gather.12.cloned.1.call-update) | async-done | bytes 7864336 | tf_op jit(solution)/shard_map/all_gather | solution.py:58
  298.5 3.8 fusion.36
  302.3 8.0 fusion.20
  310.3 5.8 multiply_reduce_fusion.14
  317.3 2.7 fusion.115
  323.4 7.2 fusion.17
  363.1 3.2 fusion.55
  366.4 4.1 reshape.619
  373.7 2.8 constant_dynamic-slice_fusion.2
  384.5 2.7 convolution_bitcast_fusion.1
  396.0 7.4 fusion.10
  443.6 2.8 reshape.621
  451.2 5.4 constant_dynamic-slice_fusion
  461.6 2.8 copy.179
  464.3 3.9 convolution_bitcast_fusion
  470.7 4.1 fusion.2
  485.9 3.3 convert_bitcast_fusion
  489.2 3.3 convert_bitcast_fusion.2
  495.1 3.5 convert_bitcast_fusion.1
  498.6 3.9 pad_maximum_fusion.1
  502.6 10.7 %copy.187 = bf16[4,640,1536]{2,1,0:T(8,128)(2,1)} copy(bf16[4,640,1536]{1,2,0:T(8,128)(2,1)} %pad_maximum_fusion.1) | data formatting | bytes 15728640 | tf_op jit(solution)/shard_map/concatenate | solution.py:163
  513.3 2.7 dynamic-slice_bitcast_fusion
  516.6 6.4 collective-permute-done.10
  523.0 3.1 fusion
  527.2 3.5 convert_bitcast_fusion.3
  534.3 3.7 pad_maximum_fusion
  538.0 10.7 %copy.186 = bf16[4,640,1536]{2,1,0:T(8,128)(2,1)} copy(bf16[4,640,1536]{1,2,0:T(8,128)(2,1)} %pad_maximum_fusion) | data formatting | bytes 15728640 | tf_op jit(solution)/shard_map/concatenate | solution.py:163
  548.7 3.1 dynamic-slice_bitcast_fusion.1
  552.2 6.4 collective-permute-done.9
  558.7 3.1 fusion.1
  563.2 51.5 %reduce-scatter.21.cloned.1.call-done = bf16[320,1536]{1,0:T(8,128)(2,1)} async-done(((bf16[1280,1536]{1,0:T(8,128)(2,1)}), bf16[320,1536]{1,0:T(8,128)(2,1)}) %reduce-scatter.21.cloned.1.call-update) | async-done | bytes 983056 | tf_op jit(solution)/shard_map/reduce_scatter | solution.py:223
  616.0 4.3 all-to-all-start.1
  623.3 25.2 %all-to-all-done.1 = bf16[8,128,640]{2,1,0:T(8,128)(2,1)} async-done(((bf16[8,128,640]{2,1,0:T(8,128)(2,1)}), bf16[8,128,640]{2,1,0:T(8,128)(2,1)}, u32[]{:S(2)}, u32[]{:S(2)}) %all-to-all-start.1) | async-done | bytes 1310752 | tf_op jit(solution)/shard_map/all_to_all | solution.py:269
  648.4 3.6 all-to-all-start.3
  652.1 37.5 %reduce-scatter.17.cloned.1.call-done = bf16[320,1536]{1,0:T(8,128)(2,1)} async-done(((bf16[1280,1536]{1,0:T(8,128)(2,1)}), bf16[320,1536]{1,0:T(8,128)(2,1)}) %reduce-scatter.17.cloned.1.call-update) | async-done | bytes 983056 | tf_op jit(solution)/shard_map/reduce_scatter | solution.py:223
  689.6 25.3 %reduce-scatter.15.cloned.1.call-done = bf16[80,1152]{1,0:T(8,128)(2,1)} async-done(((bf16[320,1152]{1,0:T(8,128)(2,1)}), bf16[80,1152]{1,0:T(8,128)(2,1)}) %reduce-scatter.15.cloned.1.call-update) | async-done | bytes 184336 | tf_op jit(solution)/shard_map/reduce_scatter | solution.py:224
  714.9 24.1 %reduce-scatter.11.cloned.1.call-done = bf16[80,1152]{1,0:T(8,128)(2,1)} async-done(((bf16[320,1152]{1,0:T(8,128)(2,1)}), bf16[80,1152]{1,0:T(8,128)(2,1)}) %reduce-scatter.11.cloned.1.call-update) | async-done | bytes 184336 | tf_op jit(solution)/shard_map/reduce_scatter | solution.py:224
  744.9 21.7 %reduce-scatter.23.cloned.1.call-done = bf16[80,1536]{1,0:T(8,128)(2,1)} async-done(((bf16[320,1536]{1,0:T(8,128)(2,1)}), bf16[80,1536]{1,0:T(8,128)(2,1)}) %reduce-scatter.23.cloned.1.call-update) | async-done | bytes 245776 | tf_op jit(solution)/shard_map/reduce_scatter | solution.py:224
  766.6 27.0 %reduce-scatter.19.cloned.1.call-done = bf16[80,1536]{1,0:T(8,128)(2,1)} async-done(((bf16[320,1536]{1,0:T(8,128)(2,1)}), bf16[80,1536]{1,0:T(8,128)(2,1)}) %reduce-scatter.19.cloned.1.call-update) | async-done | bytes 245776 | tf_op jit(solution)/shard_map/reduce_scatter | solution.py:224
  (739 shorter events, 223.6 us)
Async XLA Ops:
  7.2 75.2 %all-gather.6.cloned.1.call-start = ((), (), s32[]{:S(2)}) async-start(), calls=%async_computation.12 | async-start | bytes 3379200 | tf_op jit(solution)/shard_map/all_gather | solution.py:58
  9.1 1.5 collective-permute-start
  11.3 132.3 %all-gather.10.cloned.1.call-start = ((), (), s32[]{:S(2)}) async-start(), calls=%async_computation.14 | async-start | bytes 3379200 | tf_op jit(solution)/shard_map/all_gather | solution.py:58
  12.1 209.0 %all-gather.8.cloned.1.call-start = ((), (), s32[]{:S(2)}) async-start(), calls=%async_computation.13 | async-start | bytes 8110080 | tf_op jit(solution)/shard_map/all_gather | solution.py:58
  13.3 32.4 %copy-start.96 = (bf16[4,1,256,640]{3,2,1,0:T(8,128)(2,1)S(1)}, bf16[4,1,256,640]{3,2,1,0:T(8,128)(2,1)}, u32[]{:S(2)}) copy-start(bf16[4,1,256,640]{3,2,1,0:T(8,128)(2,1)} %param.16) | copy-start | bytes 3932164
  13.3 1.6 collective-permute-start.2
  16.7 36.8 %all-to-all-start = ((bf16[4,128,640]{2,1,0:T(8,128)(2,1)}), bf16[4,128,640]{2,1,0:T(8,128)(2,1)S(1)}, u32[]{:S(2)}, u32[]{:S(2)}) async-start(bf16[4,128,640]{2,1,0:T(8,128)(2,1)} %dynamic-slice_bitcast_fusion.5), calls=%async_computation | async-start | bytes 1310720 | tf_op jit(solution)/shard_map/all_to_all | solution.py:264
  21.8 276.7 %all-gather.12.cloned.1.call-start = ((), (), s32[]{:S(2)}) async-start(), calls=%async_computation.15 | async-start | bytes 8110080 | tf_op jit(solution)/shard_map/all_gather | solution.py:58
  45.7 189.3 %copy-start.103 = (f32[512]{0:T(512)}, f32[512]{0:T(512)S(1)}, u32[]{:S(2)}) copy-start(f32[512]{0:T(512)S(1)} %get-tuple-element.154) | copy-start | bytes 6148
  48.7 36.1 %copy-start.153 = (f32[256]{0:T(256)}, f32[256]{0:T(256)S(1)}, u32[]{:S(2)}) copy-start(f32[256]{0:T(256)S(1)} %mul.1114) | copy-start | bytes 3076
  53.1 106.0 %copy-start.52 = (pred[256,512]{1,0:T(8,128)(4,1)}, pred[256,512]{1,0:T(8,128)(4,1)S(1)}, u32[]{:S(2)}) copy-start(pred[256,512]{1,0:T(8,128)(4,1)S(1)} %fusion.154) | copy-start | bytes 393220
  53.5 110.3 %copy-start.9 = (bf16[4,128,640]{2,1,0:T(8,128)(2,1)}, bf16[4,128,640]{2,1,0:T(8,128)(2,1)S(1)}, u32[]{:S(2)}) copy-start(bf16[4,128,640]{2,1,0:T(8,128)(2,1)S(1)} %all-to-all-done) | copy-start | bytes 1966084
  53.5 263.8 %all-to-all-start.2 = ((bf16[4,128,640]{2,1,0:T(8,128)(2,1)}), bf16[4,128,640]{2,1,0:T(8,128)(2,1)}, u32[]{:S(2)}, u32[]{:S(2)}) async-start(bf16[4,128,640]{2,1,0:T(8,128)(2,1)} %dynamic-slice_bitcast_fusion.4), calls=%async_computation.2 | async-start | bytes 1310720 | tf_op jit(solution)/shard_map/all_to_all | solution.py:264
  57.8 504.1 %reduce-scatter.13.cloned.1.call-start = ((), (), s32[]{:S(2)}) async-start(), calls=%async_computation.18 | async-start | bytes 3686400 | tf_op jit(solution)/shard_map/reduce_scatter | solution.py:223
  58.0 25.9 %copy-start.129 = (f32[4,128]{1,0:T(4,128)}, f32[4,128]{1,0:T(4,128)S(1)}, u32[]{:S(2)}) copy-start(f32[4,128]{1,0:T(4,128)S(1)} %fusion.122) | copy-start | bytes 6148
  58.0 25.9 %copy-start.135 = (f32[512]{0:T(512)}, f32[512]{0:T(512)S(1)}, u32[]{:S(2)}) copy-start(f32[512]{0:T(512)S(1)} %bitcast_rsqrt_fusion) | copy-start | bytes 6148
  86.7 59.4 %copy-start.40 = (f32[512,128]{0,1:T(8,128)}, f32[512,128]{0,1:T(8,128)S(1)}, u32[]{:S(2)}) copy-start(f32[512,128]{0,1:T(8,128)S(1)} %get-tuple-element.111) | copy-start | bytes 786436
  86.7 59.4 %copy-start.44 = (f32[512,128]{0,1:T(8,128)}, f32[512,128]{0,1:T(8,128)S(1)}, u32[]{:S(2)}) copy-start(f32[512,128]{0,1:T(8,128)S(1)} %get-tuple-element.112) | copy-start | bytes 786436
  87.6 61.6 %collective-permute-start.1 = (bf16[512,512]{0,1:T(8,128)(2,1)}, bf16[512,512]{0,1:T(8,128)(2,1)}, u32[]{:S(2)}, u32[]{:S(2)}) collective-permute-start(bf16[512,512]{0,1:T(8,128)(2,1)} %pad_maximum_fusion.16), channel_id=1, source_target_pairs={{0,16},{16,0},{1,17},{17,1},{2,18},{18,2},{3,19},{19,3},{4,20},{20... | collective-permute-start | bytes 1572872 | tf_op jit(solution)/shard_map/ppermute | solution.py:45
  164.8 60.0 %copy-start.143 = (f32[512]{0:T(512)}, f32[512]{0:T(512)S(1)}, u32[]{:S(2)}) copy-start(f32[512]{0:T(512)S(1)} %get-tuple-element.46) | copy-start | bytes 6148
  164.8 60.0 %copy-start.137 = (f32[512]{0:T(512)}, f32[512]{0:T(512)S(1)}, u32[]{:S(2)}) copy-start(f32[512]{0:T(512)S(1)} %fusion.234) | copy-start | bytes 6148
  165.1 59.8 %copy-start.91 = (bf16[512,640,1]{1,0,2:T(8,128)(2,1)}, bf16[512,640,1]{1,0,2:T(8,128)(2,1)S(1)}, u32[]{:S(2)}) copy-start(bf16[512,640,1]{1,0,2:T(8,128)(2,1)S(1)} %fusion.139) | copy-start | bytes 1966084
  232.6 161.2 %copy-start.19 = (bf16[512,640]{1,0:T(8,128)(2,1)}, bf16[512,640]{1,0:T(8,128)(2,1)S(1)}, u32[]{:S(2)}) copy-start(bf16[512,640]{1,0:T(8,128)(2,1)S(1)} %get-tuple-element.45) | copy-start | bytes 1966084
  236.3 6.9 collective-permute-start.3
  320.7 9.8 %slice-start.4 = ((s8[7864320]{0:T(1024)(128)(4,1)}), s8[4194304]{0:T(1024)(128)(4,1)S(1)}, s32[]{:S(2)}) async-start(s8[7864320]{0:T(1024)(128)(4,1)} %bitcast.539), calls=%async_computation.28 | async-start | bytes 8388608
  380.4 6.8 collective-permute-start.4
  394.0 9.4 %slice-start.2 = ((s8[7864320]{0:T(1024)(128)(4,1)}), s8[4194304]{0:T(1024)(128)(4,1)S(1)}, s32[]{:S(2)}) async-start(s8[7864320]{0:T(1024)(128)(4,1)} %bitcast.531), calls=%async_computation.26 | async-start | bytes 8388608
  395.4 12.7 %copy-start.35 = (bf16[512,640]{1,0:T(8,128)(2,1)}, bf16[512,640]{1,0:T(8,128)(2,1)S(1)}, u32[]{:S(2)}) copy-start(bf16[512,640]{1,0:T(8,128)(2,1)S(1)} %get-tuple-element.40) | copy-start | bytes 1966084
  439.6 31.1 %collective-permute-start.7 = (bf16[4,4,80,1152]{3,2,1,0:T(8,128)(2,1)}, bf16[4,4,80,1152]{3,2,1,0:T(8,128)(2,1)}, u32[]{:S(2)}, u32[]{:S(2)}) collective-permute-start(bf16[4,4,80,1152]{3,2,1,0:T(8,128)(2,1)} %dynamic-slice_bitcast_fusion.2), channel_id=1, source_target_pairs={{0,16},{16,0},{1,17},{17,1},{2,18},{18,2},{3,19},{19,3},{4,20},{20... | collective-permute-start | bytes 8847368 | tf_op jit(solution)/shard_map/ppermute | solution.py:45
  457.6 10.6 %collective-permute-start.5 = (bf16[4,128,512]{1,0,2:T(4,128)(2,1)}, bf16[4,128,512]{1,0,2:T(4,128)(2,1)}, u32[]{:S(2)}, u32[]{:S(2)}) collective-permute-start(bf16[4,128,512]{1,0,2:T(4,128)(2,1)} %convert_bitcast_fusion.6), channel_id=1, source_target_pairs={{0,16},{16,0},{1,17},{17,1},{2,18},{18,2},{3,19},{19,3},{4,20},{20... | collective-permute-start | bytes 1572872 | tf_op jit(solution)/shard_map/ppermute | solution.py:45
  474.9 87.8 %reduce-scatter.9.cloned.1.call-start = ((), (), s32[]{:S(2)}) async-start(), calls=%async_computation.16 | async-start | bytes 3686400 | tf_op jit(solution)/shard_map/reduce_scatter | solution.py:223
  484.4 8.2 %collective-permute-start.6 = (bf16[4,4,80,1152]{3,2,1,0:T(8,128)(2,1)S(1)}, bf16[4,4,80,1152]{3,2,1,0:T(8,128)(2,1)S(1)}, u32[]{:S(2)}, u32[]{:S(2)}) collective-permute-start(bf16[4,4,80,1152]{3,2,1,0:T(8,128)(2,1)S(1)} %dynamic-slice_bitcast_fusion.3), channel_id=1, source_target_pairs={{0,16},{16,0},{1,17},{17,1},{2,18},{18,2},{3,19},{19,3},{4,20},{20... | collective-permute-start | bytes 8847368 | tf_op jit(solution)/shard_map/ppermute | solution.py:45
  495.0 119.7 %reduce-scatter.21.cloned.1.call-start = ((), (), s32[]{:S(2)}) async-start(), calls=%async_computation.22 | async-start | bytes 4915200 | tf_op jit(solution)/shard_map/reduce_scatter | solution.py:223
  513.3 9.7 %copy-start.7 = (bf16[4,640,1536]{2,1,0:T(8,128)(2,1)S(1)}, bf16[4,640,1536]{2,1,0:T(8,128)(2,1)}, u32[]{:S(2)}) copy-start(bf16[4,640,1536]{2,1,0:T(8,128)(2,1)} %copy.187) | copy-start | bytes 23592964
  515.9 7.0 collective-permute-start.10
  526.1 163.5 %reduce-scatter.17.cloned.1.call-start = ((), (), s32[]{:S(2)}) async-start(), calls=%async_computation.20 | async-start | bytes 4915200 | tf_op jit(solution)/shard_map/reduce_scatter | solution.py:223
  548.7 10.0 %copy-start.6 = (bf16[4,640,1536]{2,1,0:T(8,128)(2,1)S(1)}, bf16[4,640,1536]{2,1,0:T(8,128)(2,1)}, u32[]{:S(2)}) copy-start(bf16[4,640,1536]{2,1,0:T(8,128)(2,1)} %copy.186) | copy-start | bytes 23592964
  551.8 6.8 collective-permute-start.9
  561.8 52.9 %copy-start.20 = (bf16[512,640]{1,0:T(8,128)(2,1)S(1)}, bf16[512,640]{1,0:T(8,128)(2,1)}, u32[]{:S(2)}) copy-start(bf16[512,640]{1,0:T(8,128)(2,1)} %copy-done.19) | copy-start | bytes 1966084
  561.9 52.9 %copy-start.71 = (bf16[1,512,640]{2,1,0:T(8,128)(2,1)S(1)}, bf16[1,512,640]{2,1,0:T(8,128)(2,1)}, u32[]{:S(2)}) copy-start(bf16[1,512,640]{2,1,0:T(8,128)(2,1)} %get-tuple-element.65) | copy-start | bytes 1966084
  561.9 153.0 %reduce-scatter.15.cloned.1.call-start = ((), (), s32[]{:S(2)}) async-start(), calls=%async_computation.19 | async-start | bytes 921600 | tf_op jit(solution)/shard_map/reduce_scatter | solution.py:224
  562.6 176.4 %reduce-scatter.11.cloned.1.call-start = ((), (), s32[]{:S(2)}) async-start(), calls=%async_computation.17 | async-start | bytes 921600 | tf_op jit(solution)/shard_map/reduce_scatter | solution.py:224
  563.2 203.4 %reduce-scatter.23.cloned.1.call-start = ((), (), s32[]{:S(2)}) async-start(), calls=%async_computation.23 | async-start | bytes 1228800 | tf_op jit(solution)/shard_map/reduce_scatter | solution.py:224
  616.0 32.5 %all-to-all-start.1 = ((bf16[8,128,640]{2,1,0:T(8,128)(2,1)}), bf16[8,128,640]{2,1,0:T(8,128)(2,1)}, u32[]{:S(2)}, u32[]{:S(2)}) async-start(bf16[8,128,640]{2,1,0:T(8,128)(2,1)} %bitcast.482), calls=%async_computation.1 | async-start | bytes 2621440 | tf_op jit(solution)/shard_map/all_to_all | solution.py:269
  648.4 94.1 %all-to-all-start.3 = ((bf16[8,128,640]{2,1,0:T(8,128)(2,1)}), bf16[8,128,640]{2,1,0:T(8,128)(2,1)S(1)}, u32[]{:S(2)}, u32[]{:S(2)}) async-start(bf16[8,128,640]{2,1,0:T(8,128)(2,1)} %bitcast.84), calls=%async_computation.3 | async-start | bytes 2621440 | tf_op jit(solution)/shard_map/all_to_all | solution.py:269
  652.0 141.6 %reduce-scatter.19.cloned.1.call-start = ((), (), s32[]{:S(2)}) async-start(), calls=%async_computation.21 | async-start | bytes 1228800 | tf_op jit(solution)/shard_map/reduce_scatter | solution.py:224
  739.9 4.3 collective-permute-start.8
  794.6 1.6 collective-permute-start.11
  (203 other events, 583.9 us)
Sparse Core Ops, SparseCore 0:
  11.5 70.8 all-gather.5
  85.8 57.8 all-gather.9
  146.7 74.3 all-gather.7
  224.5 73.9 all-gather.11
  475.0 40.8 reduce-scatter.12
  518.8 42.2 reduce-scatter.8
  564.1 50.5 reduce-scatter.20
  617.8 71.7 reduce-scatter.16
  691.9 22.9 reduce-scatter.14
  717.0 21.9 reduce-scatter.10
  741.3 25.2 reduce-scatter.22
  768.9 24.6 reduce-scatter.18
